TPU v7x, 32 devices: a whole 2x2x4 slice. The times are simulated.
32 devices in a mesh: blk: 8 (over y, x, core), cast: 4 (over z).
Axes of the slice: x: 2, y: 2, z: 4, core: 2. Of those that a mesh axis runs over, the one named last changes fastest.
Arguments:
- film_temp: float32 [16, 128, 2048], P(None, 'cast', 'blk'), may hold values from -6 to 6
- surface_temp: float32 [128, 2048], P('cast', 'blk'), may hold values from 0.5 to 2
- shell_enthalpy: float32 [64, 128, 2048], P('blk', 'cast'), may hold values from 0 to 3
- phase_codes: int32 [16, 64], P('cast', 'blk'), may hold values from 0 to 2
- zone_ids: int32 [8], P('cast'), may hold values from 0 to 7
- zone_htc: float32 [8], replicated, may hold values from 0.5 to 1.5
Outputs:
- film_out: float32 [16, 128, 2048], P(None, 'cast', 'blk')
- shell_out: float32 [64, 128, 2048], P('blk', 'cast')
- surface_out: float32 [128, 2048], P('cast', 'blk')
All inputs are finite; a program needn't handle non-finite values.
Results may differ from a plain program's by a relative error of at most 0.00002.
Values sent between devices are 32-bit elements; how exact they have to be, the bound alone decides.
A program may use at most 128 MiB of HBM per device.

v0:
```python
import jax
import jax.numpy as jnp
from jax import lax
from jax.sharding import PartitionSpec as P

TILE_R = 8
TILE_P = 32
ZONE_ROWS = 16
ZONES = 8
FILM_SWEEPS = 4
SHELL_SWEEPS = 10


normal_gain = 2.0
advance_flux_film = 0.1
shell_step = 0.15


def with_halo(cells, sides, width, closed):
    for axis, dim in sides:
        count = lax.axis_size(axis)
        ends = count if closed else count - 1
        head = lax.slice_in_dim(cells, 0, width, axis=dim)
        tail = lax.slice_in_dim(cells, cells.shape[dim] - width, cells.shape[dim], axis=dim)
        cells = jnp.concatenate(
            [
                lax.ppermute(tail, axis, [(i, (i + 1) % count) for i in range(ends)]),
                cells,
                lax.ppermute(head, axis, [((i + 1) % count, i) for i in range(ends)]),
            ],
            axis=dim,
        )
    return cells


def broadcast(array, axis, root):
    mine = lax.axis_index(axis) == root
    return lax.psum(jnp.where(mine, array, jnp.zeros_like(array)), axis)


def tile_conductivity(phase_codes):
    values = jnp.where(phase_codes == 0, 1.0, jnp.where(phase_codes == 1, 0.55, 0.3)).astype(
        jnp.float32
    )
    count_r, count_p = values.shape
    spread = jnp.broadcast_to(values[:, None, :, None], (count_r, TILE_R, count_p, TILE_P))
    return spread.reshape(count_r * TILE_R, count_p * TILE_P)


def row_cooling(zone_ids, zone_htc):
    onehot = (zone_ids[:, None] == jnp.arange(ZONES, dtype=jnp.int32)[None, :]).astype(
        zone_htc.dtype
    )
    per_block = jnp.sum(onehot * zone_htc[None, :], axis=1)
    return jnp.repeat(per_block, ZONE_ROWS)


def thermal_map(heat_content_per_mass):
    return jnp.minimum(heat_content_per_mass, 1.0) + jnp.maximum(heat_content_per_mass - 2.0, 0.0)


def film_update(film, sideways_conduction, conduct, cooling, crust_outer_face):
    below = jnp.concatenate([film[:1], film[:-1]], 0)
    above = jnp.concatenate([film[1:], crust_outer_face[None]], 0)
    normal = normal_gain * conduct * (above + below - 2.0 * film)
    normal = normal.at[0].add(-cooling[:, None] * film[0])
    return film + advance_flux_film * (conduct * sideways_conduction + normal)


def mirror_ends(forward_neighbour, trailing_neighbour, field, position, extent, dim):
    length = field.shape[dim]
    ahead_end = jnp.where(
        position == extent - 1,
        lax.slice_in_dim(field, length - 1, length, axis=dim),
        lax.slice_in_dim(forward_neighbour, length - 1, length, axis=dim),
    )
    forward_neighbour = jnp.concatenate(
        [lax.slice_in_dim(forward_neighbour, 0, length - 1, axis=dim), ahead_end], axis=dim
    )
    behind_end = jnp.where(
        position == 0,
        lax.slice_in_dim(field, 0, 1, axis=dim),
        lax.slice_in_dim(trailing_neighbour, 0, 1, axis=dim),
    )
    trailing_neighbour = jnp.concatenate(
        [behind_end, lax.slice_in_dim(trailing_neighbour, 1, length, axis=dim)], axis=dim
    )
    return (forward_neighbour, trailing_neighbour)


def body(film_temp, surface_temp, shell_enthalpy, phase_codes, zone_ids, zone_htc):
    conduct = tile_conductivity(phase_codes)
    cooling = row_cooling(zone_ids, zone_htc)
    width = film_temp.shape[2]
    tile_position = lax.axis_index("blk")
    number_of_tiles = lax.axis_size("blk")
    strand_number = lax.axis_index("cast")
    number_of_strands = lax.axis_size("cast")
    film = film_temp
    for sweep in range(FILM_SWEEPS):
        cycle = with_halo(film, (("blk", 2),), 1, True)
        rows = with_halo(film, (("cast", 1),), 1, False)
        forward_neighbour, trailing_neighbour = mirror_ends(
            rows[:, 2:], rows[:, :-2], film, strand_number, number_of_strands, 1
        )
        sideways_conduction = (
            forward_neighbour + trailing_neighbour + cycle[:, :, 2:] + cycle[:, :, :-2] - 4.0 * film
        )
        film = film_update(film, sideways_conduction, conduct, cooling, surface_temp)
    flux = normal_gain * conduct * (film[-1] - surface_temp)
    plane = lax.all_gather(flux, "blk", axis=1, tiled=True)
    heating = jnp.where(tile_position == 0, shell_step * plane, 0.0)

    def sweep_depth(step, heat_content_per_mass):
        pointwise_heat_level = thermal_map(heat_content_per_mass)
        widened_array = with_halo(pointwise_heat_level, (("blk", 0), ("cast", 1)), 1, False)
        inner_neighbour, outer_neighbour = mirror_ends(
            widened_array[2:, 1:-1],
            widened_array[:-2, 1:-1],
            pointwise_heat_level,
            tile_position,
            number_of_tiles,
            0,
        )
        forward_neighbour, trailing_neighbour = mirror_ends(
            widened_array[1:-1, 2:],
            widened_array[1:-1, :-2],
            pointwise_heat_level,
            strand_number,
            number_of_strands,
            1,
        )
        iteration_counter = (
            inner_neighbour
            + outer_neighbour
            + forward_neighbour
            + trailing_neighbour
            + jnp.roll(pointwise_heat_level, 1, 2)
            + jnp.roll(pointwise_heat_level, -1, 2)
            - 6.0 * pointwise_heat_level
        )
        heat_content_per_mass = heat_content_per_mass + shell_step * iteration_counter
        return heat_content_per_mass.at[0].add(heating)

    frozen_crust = lax.fori_loop(0, SHELL_SWEEPS, sweep_depth, shell_enthalpy)
    whole_region = broadcast(thermal_map(frozen_crust[0]), "blk", 0)
    crust_outer_face = lax.dynamic_slice_in_dim(whole_region, tile_position * width, width, 1)
    return (film, frozen_crust, crust_outer_face)


def solution(mesh):
    placed = (
        P(None, "cast", "blk"),
        P("cast", "blk"),
        P("blk", "cast", None),
        P("cast", "blk"),
        P("cast"),
        P(),
    )
    return jax.shard_map(
        body,
        mesh=mesh,
        in_specs=placed,
        out_specs=(P(None, "cast", "blk"), P("blk", "cast", None), P("cast", "blk")),
        check_vma=False,
    )
```

profile of v0, /device:TPU:0, one launch (start us, length us, event | category | flops | bytes accessed | tf_op | source)
XLA Modules:
  0.0 461.7 jit_solution(2153601367095982840)
XLA Ops:
  7.2 3.2 copy.22
  10.4 4.9 %collective-permute-start.5 = (f32[16,1,256]{2,1,0:T(1,128)S(1)}, f32[16,1,256]{2,1,0:T(1,128)S(1)}, u32[]{:S(2)}, u32[]{:S(2)}) collective-permute-start(f32[16,1,256]{2,1,0:T(1,128)S(1)} %get-tuple-element.206), channel_id=1, source_target_pairs={{0,1},{1,2},{2,3},{4,5},{5,6},{6,7},{8,9},{9,10},{10,11},{12,13},{... | collective-permute-start | bytes 49160 | tf_op jit(solution)/shard_map/ppermute | solution.py:27
  21.0 4.5 collective-permute-done.6
  29.2 4.5 collective-permute-start.9
  35.8 3.6 collective-permute-done.8
  44.0 4.5 collective-permute-start.13
  51.2 3.0 collective-permute-done.12
  59.1 4.5 collective-permute-start.17
  66.3 3.0 collective-permute-done.16
  74.1 8.3 %all_gather.3 = f32[32,2048]{1,0:T(8,128)S(1)} all-gather(f32[32,256]{1,0:T(8,128)S(1)} %fusion.49), channel_id=1, replica_groups=mesh['blk'=8,'cast'=4] {'blk'}, dimensions={1}, use_global_device_ids=true | all-gather | bytes 294912 | tf_op jit(solution)/shard_map/all_gather | solution.py:111
  82.5 309.9 %while.17 = (s32[]{:T(128)}, f32[8,32,2048]{2,1,0:T(8,128)}, pred[]{:T(512)}, pred[]{:T(512)}, pred[]{:T(512)}, /*index=5*/pred[]{:T(512)}, f32[32,2048]{1,0:T(8,128)S(1)}, s32[]{:T(128)}) while((s32[]{:T(128)}, f32[8,32,2048]{2,1,0:T(8,128)}, pred[]{:T(512)}, pred[]{:T(512)}, pred[]{:T(512)}, /*index=5*/pred[]{:T(512)}, ...), condition=%wide.region_2.3_spmd, body=%wide.region_1.2_spmd.sunk | while | flops 12369922 | bytes 79327568 | solution.py:145
  88.0 2.7 fusion.86
  95.7 4.8 %collective-permute-start.2 = (f32[10,1,2048]{2,1,0:T(1,128)S(1)}, f32[10,1,2048]{2,1,0:T(1,128)S(1)}, u32[]{:S(2)}, u32[]{:S(2)}) collective-permute-start(f32[10,1,2048]{2,1,0:T(1,128)S(1)} %get-tuple-element.279), channel_id=1, source_target_pairs={{0,1},{1,2},{2,3},{4,5},{5,6},{6,7},{8,9},{9,10},{10,11},{12,13},{... | collective-permute-start | bytes 245768 | tf_op jit(solution)/shard_map/while/body/eval_jaxpr/ppermute | solution.py:27
  102.6 4.6 collective-permute-done.3
  107.4 5.1 %fusion.88 = f32[8,32,2048]{2,1,0:T(8,128)S(1)} fusion(f32[8,32,2048]{2,1,0:T(8,128)S(1)} %copy-done, f32[1,32,2048]{2,1,0:T(8,128)S(1)} %get-tuple-element.275, f32[7,32,2048]{2,1,0:T(8,128)} %get-tuple-element.276, f32[7,32,2048]{2,1,0:T(8,128)} %get-tuple-element.277, f32[1,32,2048]{2,1,0:T(8,128)S(1)} %get-tuple-element.278, ...), kind=kLoop, calls=%fused_computation.7.clone.1 | loop fusion | flops 9961472 | bytes 16777216 | tf_op jit(solution)/shard_map/while/body/eval_jaxpr/add | solution.py:142
  119.4 2.7 fusion.86
  127.0 3.8 collective-permute-start.2
  132.8 4.3 collective-permute-done.3
  137.3 5.1 %fusion.88 = f32[8,32,2048]{2,1,0:T(8,128)S(1)} fusion(f32[8,32,2048]{2,1,0:T(8,128)S(1)} %copy-done, f32[1,32,2048]{2,1,0:T(8,128)S(1)} %get-tuple-element.275, f32[7,32,2048]{2,1,0:T(8,128)} %get-tuple-element.276, f32[7,32,2048]{2,1,0:T(8,128)} %get-tuple-element.277, f32[1,32,2048]{2,1,0:T(8,128)S(1)} %get-tuple-element.278, ...), kind=kLoop, calls=%fused_computation.7.clone.1 | loop fusion | flops 9961472 | bytes 16777216 | tf_op jit(solution)/shard_map/while/body/eval_jaxpr/add | solution.py:142
  145.7 4.0 collective-permute-start
  151.0 2.7 fusion.86
  158.7 3.7 collective-permute-start.2
  164.5 4.3 collective-permute-done.3
  169.0 5.1 %fusion.88 = f32[8,32,2048]{2,1,0:T(8,128)S(1)} fusion(f32[8,32,2048]{2,1,0:T(8,128)S(1)} %copy-done, f32[1,32,2048]{2,1,0:T(8,128)S(1)} %get-tuple-element.275, f32[7,32,2048]{2,1,0:T(8,128)} %get-tuple-element.276, f32[7,32,2048]{2,1,0:T(8,128)} %get-tuple-element.277, f32[1,32,2048]{2,1,0:T(8,128)S(1)} %get-tuple-element.278, ...), kind=kLoop, calls=%fused_computation.7.clone.1 | loop fusion | flops 9961472 | bytes 16777216 | tf_op jit(solution)/shard_map/while/body/eval_jaxpr/add | solution.py:142
  177.4 4.6 %collective-permute-start = (f32[1,32,2048]{2,1,0:T(8,128)S(1)}, f32[1,32,2048]{2,1,0:T(8,128)S(1)}, u32[]{:S(2)}, u32[]{:S(2)}) collective-permute-start(f32[1,32,2048]{2,1,0:T(8,128)S(1)} %get-tuple-element.273), channel_id=1, source_target_pairs={{0,4},{4,8},{8,12},{12,16},{16,20},{20,24},{24,28},{1,5},{5,9},{9,... | collective-permute-start | bytes 786440 | tf_op jit(solution)/shard_map/while/body/eval_jaxpr/ppermute | solution.py:27
  183.3 2.7 fusion.86
  195.5 4.3 collective-permute-done.3
  200.0 5.1 %fusion.88 = f32[8,32,2048]{2,1,0:T(8,128)S(1)} fusion(f32[8,32,2048]{2,1,0:T(8,128)S(1)} %copy-done, f32[1,32,2048]{2,1,0:T(8,128)S(1)} %get-tuple-element.275, f32[7,32,2048]{2,1,0:T(8,128)} %get-tuple-element.276, f32[7,32,2048]{2,1,0:T(8,128)} %get-tuple-element.277, f32[1,32,2048]{2,1,0:T(8,128)S(1)} %get-tuple-element.278, ...), kind=kLoop, calls=%fused_computation.7.clone.1 | loop fusion | flops 9961472 | bytes 16777216 | tf_op jit(solution)/shard_map/while/body/eval_jaxpr/add | solution.py:142
  208.4 5.1 %collective-permute-start = (f32[1,32,2048]{2,1,0:T(8,128)S(1)}, f32[1,32,2048]{2,1,0:T(8,128)S(1)}, u32[]{:S(2)}, u32[]{:S(2)}) collective-permute-start(f32[1,32,2048]{2,1,0:T(8,128)S(1)} %get-tuple-element.273), channel_id=1, source_target_pairs={{0,4},{4,8},{8,12},{12,16},{16,20},{20,24},{24,28},{1,5},{5,9},{9,... | collective-permute-start | bytes 786440 | tf_op jit(solution)/shard_map/while/body/eval_jaxpr/ppermute | solution.py:27
  214.8 2.7 fusion.86
  227.0 4.3 collective-permute-done.3
  231.5 5.1 %fusion.88 = f32[8,32,2048]{2,1,0:T(8,128)S(1)} fusion(f32[8,32,2048]{2,1,0:T(8,128)S(1)} %copy-done, f32[1,32,2048]{2,1,0:T(8,128)S(1)} %get-tuple-element.275, f32[7,32,2048]{2,1,0:T(8,128)} %get-tuple-element.276, f32[7,32,2048]{2,1,0:T(8,128)} %get-tuple-element.277, f32[1,32,2048]{2,1,0:T(8,128)S(1)} %get-tuple-element.278, ...), kind=kLoop, calls=%fused_computation.7.clone.1 | loop fusion | flops 9961472 | bytes 16777216 | tf_op jit(solution)/shard_map/while/body/eval_jaxpr/add | solution.py:142
  239.9 4.8 %collective-permute-start = (f32[1,32,2048]{2,1,0:T(8,128)S(1)}, f32[1,32,2048]{2,1,0:T(8,128)S(1)}, u32[]{:S(2)}, u32[]{:S(2)}) collective-permute-start(f32[1,32,2048]{2,1,0:T(8,128)S(1)} %get-tuple-element.273), channel_id=1, source_target_pairs={{0,4},{4,8},{8,12},{12,16},{16,20},{20,24},{24,28},{1,5},{5,9},{9,... | collective-permute-start | bytes 786440 | tf_op jit(solution)/shard_map/while/body/eval_jaxpr/ppermute | solution.py:27
  258.1 4.3 collective-permute-done.3
  262.6 5.1 %fusion.88 = f32[8,32,2048]{2,1,0:T(8,128)S(1)} fusion(f32[8,32,2048]{2,1,0:T(8,128)S(1)} %copy-done, f32[1,32,2048]{2,1,0:T(8,128)S(1)} %get-tuple-element.275, f32[7,32,2048]{2,1,0:T(8,128)} %get-tuple-element.276, f32[7,32,2048]{2,1,0:T(8,128)} %get-tuple-element.277, f32[1,32,2048]{2,1,0:T(8,128)S(1)} %get-tuple-element.278, ...), kind=kLoop, calls=%fused_computation.7.clone.1 | loop fusion | flops 9961472 | bytes 16777216 | tf_op jit(solution)/shard_map/while/body/eval_jaxpr/add | solution.py:142
  271.0 4.7 %collective-permute-start = (f32[1,32,2048]{2,1,0:T(8,128)S(1)}, f32[1,32,2048]{2,1,0:T(8,128)S(1)}, u32[]{:S(2)}, u32[]{:S(2)}) collective-permute-start(f32[1,32,2048]{2,1,0:T(8,128)S(1)} %get-tuple-element.273), channel_id=1, source_target_pairs={{0,4},{4,8},{8,12},{12,16},{16,20},{20,24},{24,28},{1,5},{5,9},{9,... | collective-permute-start | bytes 786440 | tf_op jit(solution)/shard_map/while/body/eval_jaxpr/ppermute | solution.py:27
  289.2 4.3 collective-permute-done.3
  293.7 5.1 %fusion.88 = f32[8,32,2048]{2,1,0:T(8,128)S(1)} fusion(f32[8,32,2048]{2,1,0:T(8,128)S(1)} %copy-done, f32[1,32,2048]{2,1,0:T(8,128)S(1)} %get-tuple-element.275, f32[7,32,2048]{2,1,0:T(8,128)} %get-tuple-element.276, f32[7,32,2048]{2,1,0:T(8,128)} %get-tuple-element.277, f32[1,32,2048]{2,1,0:T(8,128)S(1)} %get-tuple-element.278, ...), kind=kLoop, calls=%fused_computation.7.clone.1 | loop fusion | flops 9961472 | bytes 16777216 | tf_op jit(solution)/shard_map/while/body/eval_jaxpr/add | solution.py:142
  302.1 4.7 %collective-permute-start = (f32[1,32,2048]{2,1,0:T(8,128)S(1)}, f32[1,32,2048]{2,1,0:T(8,128)S(1)}, u32[]{:S(2)}, u32[]{:S(2)}) collective-permute-start(f32[1,32,2048]{2,1,0:T(8,128)S(1)} %get-tuple-element.273), channel_id=1, source_target_pairs={{0,4},{4,8},{8,12},{12,16},{16,20},{20,24},{24,28},{1,5},{5,9},{9,... | collective-permute-start | bytes 786440 | tf_op jit(solution)/shard_map/while/body/eval_jaxpr/ppermute | solution.py:27
  320.2 4.3 collective-permute-done.3
  324.7 5.1 %fusion.88 = f32[8,32,2048]{2,1,0:T(8,128)S(1)} fusion(f32[8,32,2048]{2,1,0:T(8,128)S(1)} %copy-done, f32[1,32,2048]{2,1,0:T(8,128)S(1)} %get-tuple-element.275, f32[7,32,2048]{2,1,0:T(8,128)} %get-tuple-element.276, f32[7,32,2048]{2,1,0:T(8,128)} %get-tuple-element.277, f32[1,32,2048]{2,1,0:T(8,128)S(1)} %get-tuple-element.278, ...), kind=kLoop, calls=%fused_computation.7.clone.1 | loop fusion | flops 9961472 | bytes 16777216 | tf_op jit(solution)/shard_map/while/body/eval_jaxpr/add | solution.py:142
  333.1 4.8 %collective-permute-start = (f32[1,32,2048]{2,1,0:T(8,128)S(1)}, f32[1,32,2048]{2,1,0:T(8,128)S(1)}, u32[]{:S(2)}, u32[]{:S(2)}) collective-permute-start(f32[1,32,2048]{2,1,0:T(8,128)S(1)} %get-tuple-element.273), channel_id=1, source_target_pairs={{0,4},{4,8},{8,12},{12,16},{16,20},{20,24},{24,28},{1,5},{5,9},{9,... | collective-permute-start | bytes 786440 | tf_op jit(solution)/shard_map/while/body/eval_jaxpr/ppermute | solution.py:27
  351.3 4.3 collective-permute-done.3
  355.8 5.1 %fusion.88 = f32[8,32,2048]{2,1,0:T(8,128)S(1)} fusion(f32[8,32,2048]{2,1,0:T(8,128)S(1)} %copy-done, f32[1,32,2048]{2,1,0:T(8,128)S(1)} %get-tuple-element.275, f32[7,32,2048]{2,1,0:T(8,128)} %get-tuple-element.276, f32[7,32,2048]{2,1,0:T(8,128)} %get-tuple-element.277, f32[1,32,2048]{2,1,0:T(8,128)S(1)} %get-tuple-element.278, ...), kind=kLoop, calls=%fused_computation.7.clone.1 | loop fusion | flops 9961472 | bytes 16777216 | tf_op jit(solution)/shard_map/while/body/eval_jaxpr/add | solution.py:142
  364.2 3.8 collective-permute-start
  381.5 4.3 collective-permute-done.3
  386.0 5.1 %fusion.88 = f32[8,32,2048]{2,1,0:T(8,128)S(1)} fusion(f32[8,32,2048]{2,1,0:T(8,128)S(1)} %copy-done, f32[1,32,2048]{2,1,0:T(8,128)S(1)} %get-tuple-element.275, f32[7,32,2048]{2,1,0:T(8,128)} %get-tuple-element.276, f32[7,32,2048]{2,1,0:T(8,128)} %get-tuple-element.277, f32[1,32,2048]{2,1,0:T(8,128)S(1)} %get-tuple-element.278, ...), kind=kLoop, calls=%fused_computation.7.clone.1 | loop fusion | flops 9961472 | bytes 16777216 | tf_op jit(solution)/shard_map/while/body/eval_jaxpr/add | solution.py:142
  394.1 59.3 %all-reduce.2.cloned.1.call-done = f32[32,2048]{1,0:T(8,128)} async-done(((f32[32,2048]{1,0:T(8,128)}), f32[32,2048]{1,0:T(8,128)}) %all-reduce.2.cloned.1.call-update) | async-done | bytes 262160 | tf_op jit(solution)/shard_map/psum | solution.py:38
  (301 shorter events, 185.7 us)
Async XLA Ops:
  7.2 446.3 %all-reduce.2.cloned.1.call-start = ((), (), s32[]{:S(2)}) async-start(), calls=%async_computation | async-start | bytes 524288 | tf_op jit(solution)/shard_map/psum | solution.py:38
  10.4 9.7 %collective-permute-start.5 = (f32[16,1,256]{2,1,0:T(1,128)S(1)}, f32[16,1,256]{2,1,0:T(1,128)S(1)}, u32[]{:S(2)}, u32[]{:S(2)}) collective-permute-start(f32[16,1,256]{2,1,0:T(1,128)S(1)} %get-tuple-element.206), channel_id=1, source_target_pairs={{0,1},{1,2},{2,3},{4,5},{5,6},{6,7},{8,9},{9,10},{10,11},{12,13},{... | collective-permute-start | bytes 49160 | tf_op jit(solution)/shard_map/ppermute | solution.py:27
  15.4 5.6 %collective-permute-start.4 = (f32[16,1,256]{2,1,0:T(1,128)S(1)}, f32[16,1,256]{2,1,0:T(1,128)S(1)}, u32[]{:S(2)}, u32[]{:S(2)}) collective-permute-start(f32[16,1,256]{2,1,0:T(1,128)S(1)} %get-tuple-element.207), channel_id=1, source_target_pairs={{1,0},{2,1},{3,2},{5,4},{6,5},{7,6},{9,8},{10,9},{11,10},{13,12},{... | collective-permute-start | bytes 49160 | tf_op jit(solution)/shard_map/ppermute | solution.py:29
  17.5 8.0 %collective-permute-start.6 = (f32[16,32,1]{2,1,0:T(8,128)}, f32[16,32,1]{2,1,0:T(8,128)S(1)}, u32[]{:S(2)}, u32[]{:S(2)}) collective-permute-start(f32[16,32,1]{2,1,0:T(8,128)} %get-tuple-element.210), channel_id=1, source_target_pairs={{4,0},{8,4},{12,8},{16,12},{20,16},{24,20},{28,24},{0,28},{5,1},{9... | collective-permute-start | bytes 6152 | tf_op jit(solution)/shard_map/ppermute | solution.py:29
  19.1 8.3 %collective-permute-start.7 = (f32[16,32,1]{2,1,0:T(8,128)}, f32[16,32,1]{2,1,0:T(8,128)}, u32[]{:S(2)}, u32[]{:S(2)}) collective-permute-start(f32[16,32,1]{2,1,0:T(8,128)} %get-tuple-element.211), channel_id=1, source_target_pairs={{0,4},{4,8},{8,12},{12,16},{16,20},{20,24},{24,28},{28,0},{1,5},{5... | collective-permute-start | bytes 6152 | tf_op jit(solution)/shard_map/ppermute | solution.py:27
  29.2 6.6 %collective-permute-start.9 = (f32[16,1,256]{2,1,0:T(1,128)S(1)}, f32[16,1,256]{2,1,0:T(1,128)S(1)}, u32[]{:S(2)}, u32[]{:S(2)}) collective-permute-start(f32[16,1,256]{2,1,0:T(1,128)S(1)} %get-tuple-element.196), channel_id=1, source_target_pairs={{0,1},{1,2},{2,3},{4,5},{5,6},{6,7},{8,9},{9,10},{10,11},{12,13},{... | collective-permute-start | bytes 49160 | tf_op jit(solution)/shard_map/ppermute | solution.py:27
  33.8 5.6 %collective-permute-start.8 = (f32[16,1,256]{2,1,0:T(1,128)S(1)}, f32[16,1,256]{2,1,0:T(1,128)S(1)}, u32[]{:S(2)}, u32[]{:S(2)}) collective-permute-start(f32[16,1,256]{2,1,0:T(1,128)S(1)} %get-tuple-element.197), channel_id=1, source_target_pairs={{1,0},{2,1},{3,2},{5,4},{6,5},{7,6},{9,8},{10,9},{11,10},{13,12},{... | collective-permute-start | bytes 49160 | tf_op jit(solution)/shard_map/ppermute | solution.py:29
  35.1 6.6 %collective-permute-start.10 = (f32[16,32,1]{2,1,0:T(8,128)S(1)}, f32[16,32,1]{2,1,0:T(8,128)S(1)}, u32[]{:S(2)}, u32[]{:S(2)}) collective-permute-start(f32[16,32,1]{2,1,0:T(8,128)S(1)} %get-tuple-element.200), channel_id=1, source_target_pairs={{4,0},{8,4},{12,8},{16,12},{20,16},{24,20},{28,24},{0,28},{5,1},{9... | collective-permute-start | bytes 6152 | tf_op jit(solution)/shard_map/ppermute | solution.py:29
  35.6 7.5 %collective-permute-start.11 = (f32[16,32,1]{2,1,0:T(8,128)S(1)}, f32[16,32,1]{2,1,0:T(8,128)S(1)}, u32[]{:S(2)}, u32[]{:S(2)}) collective-permute-start(f32[16,32,1]{2,1,0:T(8,128)S(1)} %get-tuple-element.201), channel_id=1, source_target_pairs={{0,4},{4,8},{8,12},{12,16},{16,20},{20,24},{24,28},{28,0},{1,5},{5... | collective-permute-start | bytes 6152 | tf_op jit(solution)/shard_map/ppermute | solution.py:27
  44.0 7.2 %collective-permute-start.13 = (f32[16,1,256]{2,1,0:T(1,128)S(1)}, f32[16,1,256]{2,1,0:T(1,128)S(1)}, u32[]{:S(2)}, u32[]{:S(2)}) collective-permute-start(f32[16,1,256]{2,1,0:T(1,128)S(1)} %get-tuple-element.186), channel_id=1, source_target_pairs={{0,1},{1,2},{2,3},{4,5},{5,6},{6,7},{8,9},{9,10},{10,11},{12,13},{... | collective-permute-start | bytes 49160 | tf_op jit(solution)/shard_map/ppermute | solution.py:27
  49.9 6.9 %collective-permute-start.14 = (f32[16,32,1]{2,1,0:T(8,128)S(1)}, f32[16,32,1]{2,1,0:T(8,128)S(1)}, u32[]{:S(2)}, u32[]{:S(2)}) collective-permute-start(f32[16,32,1]{2,1,0:T(8,128)S(1)} %get-tuple-element.190), channel_id=1, source_target_pairs={{4,0},{8,4},{12,8},{16,12},{20,16},{24,20},{28,24},{0,28},{5,1},{9... | collective-permute-start | bytes 6152 | tf_op jit(solution)/shard_map/ppermute | solution.py:29
  51.0 7.2 %collective-permute-start.15 = (f32[16,32,1]{2,1,0:T(8,128)S(1)}, f32[16,32,1]{2,1,0:T(8,128)S(1)}, u32[]{:S(2)}, u32[]{:S(2)}) collective-permute-start(f32[16,32,1]{2,1,0:T(8,128)S(1)} %get-tuple-element.191), channel_id=1, source_target_pairs={{0,4},{4,8},{8,12},{12,16},{16,20},{20,24},{24,28},{28,0},{1,5},{5... | collective-permute-start | bytes 6152 | tf_op jit(solution)/shard_map/ppermute | solution.py:27
  59.1 7.2 %collective-permute-start.17 = (f32[16,1,256]{2,1,0:T(1,128)S(1)}, f32[16,1,256]{2,1,0:T(1,128)S(1)}, u32[]{:S(2)}, u32[]{:S(2)}) collective-permute-start(f32[16,1,256]{2,1,0:T(1,128)S(1)} %get-tuple-element.176), channel_id=1, source_target_pairs={{0,1},{1,2},{2,3},{4,5},{5,6},{6,7},{8,9},{9,10},{10,11},{12,13},{... | collective-permute-start | bytes 49160 | tf_op jit(solution)/shard_map/ppermute | solution.py:27
  64.9 6.8 %collective-permute-start.18 = (f32[16,32,1]{2,1,0:T(8,128)S(1)}, f32[16,32,1]{2,1,0:T(8,128)S(1)}, u32[]{:S(2)}, u32[]{:S(2)}) collective-permute-start(f32[16,32,1]{2,1,0:T(8,128)S(1)} %get-tuple-element.180), channel_id=1, source_target_pairs={{4,0},{8,4},{12,8},{16,12},{20,16},{24,20},{28,24},{0,28},{5,1},{9... | collective-permute-start | bytes 6152 | tf_op jit(solution)/shard_map/ppermute | solution.py:29
  66.1 7.5 %collective-permute-start.19 = (f32[16,32,1]{2,1,0:T(8,128)S(1)}, f32[16,32,1]{2,1,0:T(8,128)S(1)}, u32[]{:S(2)}, u32[]{:S(2)}) collective-permute-start(f32[16,32,1]{2,1,0:T(8,128)S(1)} %get-tuple-element.181), channel_id=1, source_target_pairs={{0,4},{4,8},{8,12},{12,16},{16,20},{20,24},{24,28},{28,0},{1,5},{5... | collective-permute-start | bytes 6152 | tf_op jit(solution)/shard_map/ppermute | solution.py:27
  84.5 11.1 %collective-permute-start = (f32[1,32,2048]{2,1,0:T(8,128)S(1)}, f32[1,32,2048]{2,1,0:T(8,128)S(1)}, u32[]{:S(2)}, u32[]{:S(2)}) collective-permute-start(f32[1,32,2048]{2,1,0:T(8,128)S(1)} %get-tuple-element.273), channel_id=1, source_target_pairs={{0,4},{4,8},{8,12},{12,16},{16,20},{20,24},{24,28},{1,5},{5,9},{9,... | collective-permute-start | bytes 786440 | tf_op jit(solution)/shard_map/while/body/eval_jaxpr/ppermute | solution.py:27
  86.7 8.8 %collective-permute-start.1 = (f32[1,32,2048]{2,1,0:T(8,128)S(1)}, f32[1,32,2048]{2,1,0:T(8,128)S(1)}, u32[]{:S(2)}, u32[]{:S(2)}) collective-permute-start(f32[1,32,2048]{2,1,0:T(8,128)S(1)} %get-tuple-element.274), channel_id=1, source_target_pairs={{4,0},{8,4},{12,8},{16,12},{20,16},{24,20},{28,24},{5,1},{9,5},{13... | collective-permute-start | bytes 786440 | tf_op jit(solution)/shard_map/while/body/eval_jaxpr/ppermute | solution.py:29
  95.7 6.9 %collective-permute-start.2 = (f32[10,1,2048]{2,1,0:T(1,128)S(1)}, f32[10,1,2048]{2,1,0:T(1,128)S(1)}, u32[]{:S(2)}, u32[]{:S(2)}) collective-permute-start(f32[10,1,2048]{2,1,0:T(1,128)S(1)} %get-tuple-element.279), channel_id=1, source_target_pairs={{0,1},{1,2},{2,3},{4,5},{5,6},{6,7},{8,9},{9,10},{10,11},{12,13},{... | collective-permute-start | bytes 245768 | tf_op jit(solution)/shard_map/while/body/eval_jaxpr/ppermute | solution.py:27
  100.5 6.6 %collective-permute-start.3 = (f32[10,1,2048]{2,1,0:T(1,128)S(1)}, f32[10,1,2048]{2,1,0:T(1,128)S(1)}, u32[]{:S(2)}, u32[]{:S(2)}) collective-permute-start(f32[10,1,2048]{2,1,0:T(1,128)S(1)} %get-tuple-element.280), channel_id=1, source_target_pairs={{1,0},{2,1},{3,2},{5,4},{6,5},{7,6},{9,8},{10,9},{11,10},{13,12},{... | collective-permute-start | bytes 245768 | tf_op jit(solution)/shard_map/while/body/eval_jaxpr/ppermute | solution.py:29
  115.8 11.1 %collective-permute-start = (f32[1,32,2048]{2,1,0:T(8,128)S(1)}, f32[1,32,2048]{2,1,0:T(8,128)S(1)}, u32[]{:S(2)}, u32[]{:S(2)}) collective-permute-start(f32[1,32,2048]{2,1,0:T(8,128)S(1)} %get-tuple-element.273), channel_id=1, source_target_pairs={{0,4},{4,8},{8,12},{12,16},{16,20},{20,24},{24,28},{1,5},{5,9},{9,... | collective-permute-start | bytes 786440 | tf_op jit(solution)/shard_map/while/body/eval_jaxpr/ppermute | solution.py:27
  118.1 8.8 %collective-permute-start.1 = (f32[1,32,2048]{2,1,0:T(8,128)S(1)}, f32[1,32,2048]{2,1,0:T(8,128)S(1)}, u32[]{:S(2)}, u32[]{:S(2)}) collective-permute-start(f32[1,32,2048]{2,1,0:T(8,128)S(1)} %get-tuple-element.274), channel_id=1, source_target_pairs={{4,0},{8,4},{12,8},{16,12},{20,16},{24,20},{28,24},{5,1},{9,5},{13... | collective-permute-start | bytes 786440 | tf_op jit(solution)/shard_map/while/body/eval_jaxpr/ppermute | solution.py:29
  127.0 5.8 %collective-permute-start.2 = (f32[10,1,2048]{2,1,0:T(1,128)S(1)}, f32[10,1,2048]{2,1,0:T(1,128)S(1)}, u32[]{:S(2)}, u32[]{:S(2)}) collective-permute-start(f32[10,1,2048]{2,1,0:T(1,128)S(1)} %get-tuple-element.279), channel_id=1, source_target_pairs={{0,1},{1,2},{2,3},{4,5},{5,6},{6,7},{8,9},{9,10},{10,11},{12,13},{... | collective-permute-start | bytes 245768 | tf_op jit(solution)/shard_map/while/body/eval_jaxpr/ppermute | solution.py:27
  130.8 6.3 %collective-permute-start.3 = (f32[10,1,2048]{2,1,0:T(1,128)S(1)}, f32[10,1,2048]{2,1,0:T(1,128)S(1)}, u32[]{:S(2)}, u32[]{:S(2)}) collective-permute-start(f32[10,1,2048]{2,1,0:T(1,128)S(1)} %get-tuple-element.280), channel_id=1, source_target_pairs={{1,0},{2,1},{3,2},{5,4},{6,5},{7,6},{9,8},{10,9},{11,10},{13,12},{... | collective-permute-start | bytes 245768 | tf_op jit(solution)/shard_map/while/body/eval_jaxpr/ppermute | solution.py:29
  145.7 12.8 %collective-permute-start = (f32[1,32,2048]{2,1,0:T(8,128)S(1)}, f32[1,32,2048]{2,1,0:T(8,128)S(1)}, u32[]{:S(2)}, u32[]{:S(2)}) collective-permute-start(f32[1,32,2048]{2,1,0:T(8,128)S(1)} %get-tuple-element.273), channel_id=1, source_target_pairs={{0,4},{4,8},{8,12},{12,16},{16,20},{20,24},{24,28},{1,5},{5,9},{9,... | collective-permute-start | bytes 786440 | tf_op jit(solution)/shard_map/while/body/eval_jaxpr/ppermute | solution.py:27
  149.7 8.8 %collective-permute-start.1 = (f32[1,32,2048]{2,1,0:T(8,128)S(1)}, f32[1,32,2048]{2,1,0:T(8,128)S(1)}, u32[]{:S(2)}, u32[]{:S(2)}) collective-permute-start(f32[1,32,2048]{2,1,0:T(8,128)S(1)} %get-tuple-element.274), channel_id=1, source_target_pairs={{4,0},{8,4},{12,8},{16,12},{20,16},{24,20},{28,24},{5,1},{9,5},{13... | collective-permute-start | bytes 786440 | tf_op jit(solution)/shard_map/while/body/eval_jaxpr/ppermute | solution.py:29
  158.7 5.8 %collective-permute-start.2 = (f32[10,1,2048]{2,1,0:T(1,128)S(1)}, f32[10,1,2048]{2,1,0:T(1,128)S(1)}, u32[]{:S(2)}, u32[]{:S(2)}) collective-permute-start(f32[10,1,2048]{2,1,0:T(1,128)S(1)} %get-tuple-element.279), channel_id=1, source_target_pairs={{0,1},{1,2},{2,3},{4,5},{5,6},{6,7},{8,9},{9,10},{10,11},{12,13},{... | collective-permute-start | bytes 245768 | tf_op jit(solution)/shard_map/while/body/eval_jaxpr/ppermute | solution.py:27
  162.4 6.3 %collective-permute-start.3 = (f32[10,1,2048]{2,1,0:T(1,128)S(1)}, f32[10,1,2048]{2,1,0:T(1,128)S(1)}, u32[]{:S(2)}, u32[]{:S(2)}) collective-permute-start(f32[10,1,2048]{2,1,0:T(1,128)S(1)} %get-tuple-element.280), channel_id=1, source_target_pairs={{1,0},{2,1},{3,2},{5,4},{6,5},{7,6},{9,8},{10,9},{11,10},{13,12},{... | collective-permute-start | bytes 245768 | tf_op jit(solution)/shard_map/while/body/eval_jaxpr/ppermute | solution.py:29
  177.4 13.5 %collective-permute-start = (f32[1,32,2048]{2,1,0:T(8,128)S(1)}, f32[1,32,2048]{2,1,0:T(8,128)S(1)}, u32[]{:S(2)}, u32[]{:S(2)}) collective-permute-start(f32[1,32,2048]{2,1,0:T(8,128)S(1)} %get-tuple-element.273), channel_id=1, source_target_pairs={{0,4},{4,8},{8,12},{12,16},{16,20},{20,24},{24,28},{1,5},{5,9},{9,... | collective-permute-start | bytes 786440 | tf_op jit(solution)/shard_map/while/body/eval_jaxpr/ppermute | solution.py:27
  182.0 8.8 %collective-permute-start.1 = (f32[1,32,2048]{2,1,0:T(8,128)S(1)}, f32[1,32,2048]{2,1,0:T(8,128)S(1)}, u32[]{:S(2)}, u32[]{:S(2)}) collective-permute-start(f32[1,32,2048]{2,1,0:T(8,128)S(1)} %get-tuple-element.274), channel_id=1, source_target_pairs={{4,0},{8,4},{12,8},{16,12},{20,16},{24,20},{28,24},{5,1},{9,5},{13... | collective-permute-start | bytes 786440 | tf_op jit(solution)/shard_map/while/body/eval_jaxpr/ppermute | solution.py:29
  193.4 6.3 %collective-permute-start.3 = (f32[10,1,2048]{2,1,0:T(1,128)S(1)}, f32[10,1,2048]{2,1,0:T(1,128)S(1)}, u32[]{:S(2)}, u32[]{:S(2)}) collective-permute-start(f32[10,1,2048]{2,1,0:T(1,128)S(1)} %get-tuple-element.280), channel_id=1, source_target_pairs={{1,0},{2,1},{3,2},{5,4},{6,5},{7,6},{9,8},{10,9},{11,10},{13,12},{... | collective-permute-start | bytes 245768 | tf_op jit(solution)/shard_map/while/body/eval_jaxpr/ppermute | solution.py:29
  208.4 13.9 %collective-permute-start = (f32[1,32,2048]{2,1,0:T(8,128)S(1)}, f32[1,32,2048]{2,1,0:T(8,128)S(1)}, u32[]{:S(2)}, u32[]{:S(2)}) collective-permute-start(f32[1,32,2048]{2,1,0:T(8,128)S(1)} %get-tuple-element.273), channel_id=1, source_target_pairs={{0,4},{4,8},{8,12},{12,16},{16,20},{20,24},{24,28},{1,5},{5,9},{9,... | collective-permute-start | bytes 786440 | tf_op jit(solution)/shard_map/while/body/eval_jaxpr/ppermute | solution.py:27
  213.5 8.8 %collective-permute-start.1 = (f32[1,32,2048]{2,1,0:T(8,128)S(1)}, f32[1,32,2048]{2,1,0:T(8,128)S(1)}, u32[]{:S(2)}, u32[]{:S(2)}) collective-permute-start(f32[1,32,2048]{2,1,0:T(8,128)S(1)} %get-tuple-element.274), channel_id=1, source_target_pairs={{4,0},{8,4},{12,8},{16,12},{20,16},{24,20},{28,24},{5,1},{9,5},{13... | collective-permute-start | bytes 786440 | tf_op jit(solution)/shard_map/while/body/eval_jaxpr/ppermute | solution.py:29
  224.9 6.3 %collective-permute-start.3 = (f32[10,1,2048]{2,1,0:T(1,128)S(1)}, f32[10,1,2048]{2,1,0:T(1,128)S(1)}, u32[]{:S(2)}, u32[]{:S(2)}) collective-permute-start(f32[10,1,2048]{2,1,0:T(1,128)S(1)} %get-tuple-element.280), channel_id=1, source_target_pairs={{1,0},{2,1},{3,2},{5,4},{6,5},{7,6},{9,8},{10,9},{11,10},{13,12},{... | collective-permute-start | bytes 245768 | tf_op jit(solution)/shard_map/while/body/eval_jaxpr/ppermute | solution.py:29
  239.9 13.6 %collective-permute-start = (f32[1,32,2048]{2,1,0:T(8,128)S(1)}, f32[1,32,2048]{2,1,0:T(8,128)S(1)}, u32[]{:S(2)}, u32[]{:S(2)}) collective-permute-start(f32[1,32,2048]{2,1,0:T(8,128)S(1)} %get-tuple-element.273), channel_id=1, source_target_pairs={{0,4},{4,8},{8,12},{12,16},{16,20},{20,24},{24,28},{1,5},{5,9},{9,... | collective-permute-start | bytes 786440 | tf_op jit(solution)/shard_map/while/body/eval_jaxpr/ppermute | solution.py:27
  244.7 8.8 %collective-permute-start.1 = (f32[1,32,2048]{2,1,0:T(8,128)S(1)}, f32[1,32,2048]{2,1,0:T(8,128)S(1)}, u32[]{:S(2)}, u32[]{:S(2)}) collective-permute-start(f32[1,32,2048]{2,1,0:T(8,128)S(1)} %get-tuple-element.274), channel_id=1, source_target_pairs={{4,0},{8,4},{12,8},{16,12},{20,16},{24,20},{28,24},{5,1},{9,5},{13... | collective-permute-start | bytes 786440 | tf_op jit(solution)/shard_map/while/body/eval_jaxpr/ppermute | solution.py:29
  256.1 6.3 %collective-permute-start.3 = (f32[10,1,2048]{2,1,0:T(1,128)S(1)}, f32[10,1,2048]{2,1,0:T(1,128)S(1)}, u32[]{:S(2)}, u32[]{:S(2)}) collective-permute-start(f32[10,1,2048]{2,1,0:T(1,128)S(1)} %get-tuple-element.280), channel_id=1, source_target_pairs={{1,0},{2,1},{3,2},{5,4},{6,5},{7,6},{9,8},{10,9},{11,10},{13,12},{... | collective-permute-start | bytes 245768 | tf_op jit(solution)/shard_map/while/body/eval_jaxpr/ppermute | solution.py:29
  271.0 13.5 %collective-permute-start = (f32[1,32,2048]{2,1,0:T(8,128)S(1)}, f32[1,32,2048]{2,1,0:T(8,128)S(1)}, u32[]{:S(2)}, u32[]{:S(2)}) collective-permute-start(f32[1,32,2048]{2,1,0:T(8,128)S(1)} %get-tuple-element.273), channel_id=1, source_target_pairs={{0,4},{4,8},{8,12},{12,16},{16,20},{20,24},{24,28},{1,5},{5,9},{9,... | collective-permute-start | bytes 786440 | tf_op jit(solution)/shard_map/while/body/eval_jaxpr/ppermute | solution.py:27
  275.7 8.8 %collective-permute-start.1 = (f32[1,32,2048]{2,1,0:T(8,128)S(1)}, f32[1,32,2048]{2,1,0:T(8,128)S(1)}, u32[]{:S(2)}, u32[]{:S(2)}) collective-permute-start(f32[1,32,2048]{2,1,0:T(8,128)S(1)} %get-tuple-element.274), channel_id=1, source_target_pairs={{4,0},{8,4},{12,8},{16,12},{20,16},{24,20},{28,24},{5,1},{9,5},{13... | collective-permute-start | bytes 786440 | tf_op jit(solution)/shard_map/while/body/eval_jaxpr/ppermute | solution.py:29
  287.2 6.3 %collective-permute-start.3 = (f32[10,1,2048]{2,1,0:T(1,128)S(1)}, f32[10,1,2048]{2,1,0:T(1,128)S(1)}, u32[]{:S(2)}, u32[]{:S(2)}) collective-permute-start(f32[10,1,2048]{2,1,0:T(1,128)S(1)} %get-tuple-element.280), channel_id=1, source_target_pairs={{1,0},{2,1},{3,2},{5,4},{6,5},{7,6},{9,8},{10,9},{11,10},{13,12},{... | collective-permute-start | bytes 245768 | tf_op jit(solution)/shard_map/while/body/eval_jaxpr/ppermute | solution.py:29
  302.1 13.6 %collective-permute-start = (f32[1,32,2048]{2,1,0:T(8,128)S(1)}, f32[1,32,2048]{2,1,0:T(8,128)S(1)}, u32[]{:S(2)}, u32[]{:S(2)}) collective-permute-start(f32[1,32,2048]{2,1,0:T(8,128)S(1)} %get-tuple-element.273), channel_id=1, source_target_pairs={{0,4},{4,8},{8,12},{12,16},{16,20},{20,24},{24,28},{1,5},{5,9},{9,... | collective-permute-start | bytes 786440 | tf_op jit(solution)/shard_map/while/body/eval_jaxpr/ppermute | solution.py:27
  306.8 8.8 %collective-permute-start.1 = (f32[1,32,2048]{2,1,0:T(8,128)S(1)}, f32[1,32,2048]{2,1,0:T(8,128)S(1)}, u32[]{:S(2)}, u32[]{:S(2)}) collective-permute-start(f32[1,32,2048]{2,1,0:T(8,128)S(1)} %get-tuple-element.274), channel_id=1, source_target_pairs={{4,0},{8,4},{12,8},{16,12},{20,16},{24,20},{28,24},{5,1},{9,5},{13... | collective-permute-start | bytes 786440 | tf_op jit(solution)/shard_map/while/body/eval_jaxpr/ppermute | solution.py:29
  318.1 6.3 %collective-permute-start.3 = (f32[10,1,2048]{2,1,0:T(1,128)S(1)}, f32[10,1,2048]{2,1,0:T(1,128)S(1)}, u32[]{:S(2)}, u32[]{:S(2)}) collective-permute-start(f32[10,1,2048]{2,1,0:T(1,128)S(1)} %get-tuple-element.280), channel_id=1, source_target_pairs={{1,0},{2,1},{3,2},{5,4},{6,5},{7,6},{9,8},{10,9},{11,10},{13,12},{... | collective-permute-start | bytes 245768 | tf_op jit(solution)/shard_map/while/body/eval_jaxpr/ppermute | solution.py:29
  333.1 13.6 %collective-permute-start = (f32[1,32,2048]{2,1,0:T(8,128)S(1)}, f32[1,32,2048]{2,1,0:T(8,128)S(1)}, u32[]{:S(2)}, u32[]{:S(2)}) collective-permute-start(f32[1,32,2048]{2,1,0:T(8,128)S(1)} %get-tuple-element.273), channel_id=1, source_target_pairs={{0,4},{4,8},{8,12},{12,16},{16,20},{20,24},{24,28},{1,5},{5,9},{9,... | collective-permute-start | bytes 786440 | tf_op jit(solution)/shard_map/while/body/eval_jaxpr/ppermute | solution.py:27
  337.8 8.8 %collective-permute-start.1 = (f32[1,32,2048]{2,1,0:T(8,128)S(1)}, f32[1,32,2048]{2,1,0:T(8,128)S(1)}, u32[]{:S(2)}, u32[]{:S(2)}) collective-permute-start(f32[1,32,2048]{2,1,0:T(8,128)S(1)} %get-tuple-element.274), channel_id=1, source_target_pairs={{4,0},{8,4},{12,8},{16,12},{20,16},{24,20},{28,24},{5,1},{9,5},{13... | collective-permute-start | bytes 786440 | tf_op jit(solution)/shard_map/while/body/eval_jaxpr/ppermute | solution.py:29
  349.3 6.3 %collective-permute-start.3 = (f32[10,1,2048]{2,1,0:T(1,128)S(1)}, f32[10,1,2048]{2,1,0:T(1,128)S(1)}, u32[]{:S(2)}, u32[]{:S(2)}) collective-permute-start(f32[10,1,2048]{2,1,0:T(1,128)S(1)} %get-tuple-element.280), channel_id=1, source_target_pairs={{1,0},{2,1},{3,2},{5,4},{6,5},{7,6},{9,8},{10,9},{11,10},{13,12},{... | collective-permute-start | bytes 245768 | tf_op jit(solution)/shard_map/while/body/eval_jaxpr/ppermute | solution.py:29
  364.2 12.6 %collective-permute-start = (f32[1,32,2048]{2,1,0:T(8,128)S(1)}, f32[1,32,2048]{2,1,0:T(8,128)S(1)}, u32[]{:S(2)}, u32[]{:S(2)}) collective-permute-start(f32[1,32,2048]{2,1,0:T(8,128)S(1)} %get-tuple-element.273), channel_id=1, source_target_pairs={{0,4},{4,8},{8,12},{12,16},{16,20},{20,24},{24,28},{1,5},{5,9},{9,... | collective-permute-start | bytes 786440 | tf_op jit(solution)/shard_map/while/body/eval_jaxpr/ppermute | solution.py:27
  368.0 8.8 %collective-permute-start.1 = (f32[1,32,2048]{2,1,0:T(8,128)S(1)}, f32[1,32,2048]{2,1,0:T(8,128)S(1)}, u32[]{:S(2)}, u32[]{:S(2)}) collective-permute-start(f32[1,32,2048]{2,1,0:T(8,128)S(1)} %get-tuple-element.274), channel_id=1, source_target_pairs={{4,0},{8,4},{12,8},{16,12},{20,16},{24,20},{28,24},{5,1},{9,5},{13... | collective-permute-start | bytes 786440 | tf_op jit(solution)/shard_map/while/body/eval_jaxpr/ppermute | solution.py:29
  379.4 6.3 %collective-permute-start.3 = (f32[10,1,2048]{2,1,0:T(1,128)S(1)}, f32[10,1,2048]{2,1,0:T(1,128)S(1)}, u32[]{:S(2)}, u32[]{:S(2)}) collective-permute-start(f32[10,1,2048]{2,1,0:T(1,128)S(1)} %get-tuple-element.280), channel_id=1, source_target_pairs={{1,0},{2,1},{3,2},{5,4},{6,5},{7,6},{9,8},{10,9},{11,10},{13,12},{... | collective-permute-start | bytes 245768 | tf_op jit(solution)/shard_map/while/body/eval_jaxpr/ppermute | solution.py:29
  (46 other events, 268.4 us)
Sparse Core Ops, SparseCore 0:
  394.3 59.1 all-reduce.1
where the time goes:
time: 463 us; the launch traced here: 462 us
  waiting for transfers between devices  138 us (30%)
  starting transfers between devices  125 us (27%)
  local copies, waits for them, and re-layouts  95.5 us (21%)
  other arithmetic  79.3 us (17%)
  between operations  14.4 us (3%)
  blocking collectives  8.34 us (2%)
    ppermute x28, starting transfers between devices, with_halo(): lax.ppermute(tail, axis, [(i, (i + 1) % count) for i in range(ends)])  89.2 us
    ppermute x28, waiting for transfers between devices, with_halo(): lax.ppermute(head, axis, [((i + 1) % count, i) for i in range(ends)])  65.3 us
    psum x1, waiting for transfers between devices, broadcast(): return lax.psum(jnp.where(mine, array, jnp.zeros_like(array)), axis)  59.3 us
    add x10, other arithmetic, sweep_depth(): heat_content_per_mass + shell_step * iteration_counter  50.9 us
    slice x24, local copies, waits for them, and re-layouts, mirror_ends(): lax.slice_in_dim(trailing_neighbour, 1, length, axis=dim)  46.8 us
    ppermute x28, starting transfers between devices, with_halo(): lax.ppermute(head, axis, [((i + 1) % count, i) for i in range(ends)])  35.5 us
    slice x20, local copies, waits for them, and re-layouts, sweep_depth(): jnp.roll(pointwise_heat_level, -1, 2)  28.4 us
    add x10, other arithmetic, thermal_map(): jnp.minimum(heat_content_per_mass, 1.0)  18.6 us
  transfers between devices with their start and end apart: 57, of which 33 were waited for; matrix products, arithmetic and copies ran while one was open for 17% of the time, Pallas kernels for 0%

commit v1 on v0

v1 whole, which is shorter than its diff:
```python
import functools

import jax
import jax.numpy as jnp
from jax import lax
from jax.experimental import pallas as pl
from jax.experimental.pallas import tpu as pltpu
from jax.sharding import PartitionSpec as P

TILE_R = 8
TILE_P = 32
ZONE_ROWS = 16
ZONES = 8
FILM_SWEEPS = 4
SHELL_SWEEPS = 10
W = FILM_SWEEPS

normal_gain = 2.0
advance_flux_film = 0.1
shell_step = 0.15


def thermal_map(h):
    return jnp.minimum(h, 1.0) + jnp.maximum(h - 2.0, 0.0)


def remote(src, dst, send_sem, recv_sem, device):
    return pltpu.make_async_remote_copy(
        src_ref=src,
        dst_ref=dst,
        send_sem=send_sem,
        recv_sem=recv_sem,
        device_id=device,
        device_id_type=pl.DeviceIdType.MESH,
    )


def kernel(
    n,
    m,
    film_ref,
    surf_ref,
    shell_ref,
    codes_ref,
    zone_ref,
    htc_ref,
    film_out,
    shell_out,
    surf_out,
    X,
    col_out,
    col_in,
    row_out,
    row_in,
    corner_out,
    corner_in,
    corner_all,
    U,
    edge_out,
    edge_in,
    heat,
    flux_out,
    face_in,
    film_send,
    film_recv,
    flux_send,
    flux_recv,
    face_send,
    face_recv,
    depth_send,
    depth_recv,
    edge_send,
    edge_recv,
):
    b = lax.axis_index("blk")
    z = lax.axis_index("cast")
    layers, rows, width = film_ref.shape
    depth, _, perim = shell_ref.shape
    tiles = rows // 8
    full = layers + 3
    left, right = lax.rem(b + n - 1, n), lax.rem(b + 1, n)
    has_up, has_down = z > 0, z < m - 1
    has_lo, has_hi = b > 0, b < n - 1

    barrier = pltpu.get_barrier_semaphore()
    for k in range(1, n):
        pl.semaphore_signal(
            barrier, inc=1, device_id={"blk": lax.rem(b + k, n)}, device_id_type=pl.DeviceIdType.MESH
        )

    @pl.when(has_up)
    def _():
        pl.semaphore_signal(barrier, inc=1, device_id={"cast": z - 1}, device_id_type=pl.DeviceIdType.MESH)

    @pl.when(has_down)
    def _():
        pl.semaphore_signal(barrier, inc=1, device_id={"cast": z + 1}, device_id_type=pl.DeviceIdType.MESH)

    lane = lax.broadcasted_iota(jnp.int32, (8, width), 1)
    X[0:layers, 0:rows, 0:width] = film_ref[...]
    X[layers, 0:rows, 0:width] = surf_ref[...]
    for i in range(tiles):
        values = jnp.zeros((8, width), jnp.float32)
        for j in range(width // TILE_P):
            code = codes_ref[i, j]
            value = jnp.where(code == 0, 1.0, jnp.where(code == 1, 0.55, 0.3)).astype(jnp.float32)
            values = jnp.where(lane // TILE_P == j, value, values)
        X[layers + 1, 8 * i : 8 * i + 8, 0:width] = values
    for i in range(rows // ZONE_ROWS):
        zone = zone_ref[i]
        htc = jnp.float32(0.0)
        for k in range(ZONES):
            htc = htc + jnp.where(zone == k, htc_ref[k], 0.0)
        X[layers + 2, ZONE_ROWS * i : ZONE_ROWS * (i + 1), 0:width] = jnp.full(
            (ZONE_ROWS, width), htc, jnp.float32
        )
    X[:, rows : rows + 8, :] = jnp.zeros((full, 8, width + 128), jnp.float32)

    lane_r = lax.broadcasted_iota(jnp.int32, (rows, 128), 1)
    first = jnp.zeros((rows, 128), jnp.float32)
    last = jnp.zeros((rows, 128), jnp.float32)
    for l in range(full):
        mine = (lane_r >= W * l) & (lane_r < W * (l + 1))
        first = jnp.where(mine, pltpu.roll(X[l, 0:rows, 0:128], W * l, axis=1), first)
        last = jnp.where(
            mine, pltpu.roll(X[l, 0:rows, width - 128 : width], (W * l + W) % 128, axis=1), last
        )
    col_out[0] = first
    col_out[1] = last
    row_out[0] = X[:, 0:W, 0:width]
    row_out[1] = X[:, rows - W : rows, 0:width]

    pl.semaphore_wait(barrier, n - 1 + jnp.where(has_up, 1, 0) + jnp.where(has_down, 1, 0))

    col_left = remote(col_out.at[0], col_in.at[1], film_send.at[0], film_recv.at[1], {"blk": left})
    col_right = remote(col_out.at[1], col_in.at[0], film_send.at[1], film_recv.at[0], {"blk": right})
    row_up = remote(row_out.at[0], row_in.at[1], film_send.at[2], film_recv.at[3], {"cast": z - 1})
    row_down = remote(row_out.at[1], row_in.at[0], film_send.at[3], film_recv.at[2], {"cast": z + 1})
    cor_up = remote(corner_out.at[0], corner_in.at[1], film_send.at[4], film_recv.at[5], {"cast": z - 1})
    cor_down = remote(corner_out.at[1], corner_in.at[0], film_send.at[5], film_recv.at[4], {"cast": z + 1})
    col_left.start()
    col_right.start()
    pl.when(has_up)(row_up.start)
    pl.when(has_down)(row_down.start)

    def lo_copy(p, r):
        part = pl.ds(8 * r, 8)
        return remote(
            U.at[p, 1, part], U.at[p, depth + 1, part], depth_send.at[p, 0, r], depth_recv.at[p, 1, r], {"blk": b - 1}
        )

    def hi_copy(p, r):
        part = pl.ds(8 * r, 8)
        return remote(
            U.at[p, depth, part], U.at[p, 0, part], depth_send.at[p, 1, r], depth_recv.at[p, 0, r], {"blk": b + 1}
        )

    def up_copy(p):
        return remote(edge_out.at[p, 0], edge_in.at[p, 1], edge_send.at[p, 0], edge_recv.at[p, 1], {"cast": z - 1})

    def down_copy(p):
        return remote(edge_out.at[p, 1], edge_in.at[p, 0], edge_send.at[p, 1], edge_recv.at[p, 0], {"cast": z + 1})

    def lo_arrives(p, r):
        hi_copy(p, r).wait_recv()

    def hi_arrives(p, r):
        lo_copy(p, r).wait_recv()

    def first_step(d, r):
        part = pl.ds(8 * r, 8)
        h = shell_ref[d, part, :]
        shell_out[d, part, :] = h
        u = thermal_map(h)
        U[0, d + 1, part, :] = u
        if r == 0:
            edge_out[0, 0, pl.ds(d, 1), :] = u[0:1, :]
        if r == tiles - 1:
            edge_out[0, 1, pl.ds(d, 1), :] = u[7:8, :]

    for r in range(tiles):
        first_step(0, r)
        pl.when(has_lo)(lo_copy(0, r).start)
        first_step(depth - 1, r)
        pl.when(has_hi)(hi_copy(0, r).start)

    @pl.loop(1, depth - 1)
    def _(d):
        for r in range(tiles):
            first_step(d, r)

    pl.when(has_up)(up_copy(0).start)
    pl.when(has_down)(down_copy(0).start)

    col_left.wait_recv()
    col_right.wait_recv()
    corner_out[0] = col_in[:, 0:W, :]
    corner_out[1] = col_in[:, rows - W : rows, :]
    pl.when(has_up)(cor_up.start)
    pl.when(has_down)(cor_down.start)

    def unpack(l, before, after, lanes):
        after = pltpu.roll(after, (128 - W * l) % 128, axis=1)
        before = pltpu.roll(before, 128 - W - W * l, axis=1)
        zero = jnp.zeros_like(after)
        return jnp.where(lanes < W, after, jnp.where(lanes >= 128 - W, before, zero))

    for l in range(full):
        X[l, 0:rows, width : width + 128] = unpack(l, col_in[0], col_in[1], lane_r)
    corner_all[...] = jnp.zeros_like(corner_all)

    @pl.when(has_up)
    def _():
        row_down.wait_recv()
        cor_down.wait_recv()
        X[:, rows + 8 - W : rows + 8, 0:width] = row_in[0]
        corner_all[:, 8 - W : 8, :] = corner_in[0]

    @pl.when(has_down)
    def _():
        row_up.wait_recv()
        cor_up.wait_recv()
        X[:, rows : rows + W, 0:width] = row_in[1]
        corner_all[:, 0:W, :] = corner_in[1]

    for l in range(full):
        X[l, rows : rows + 8, width : width + 128] = unpack(
            l, corner_all[0], corner_all[1], lane_r[0:8]
        )

    row_id = lax.broadcasted_iota(jnp.int32, (rows + 8, width + 128), 0)
    at_top = (row_id == 0) & (z == 0)
    at_bottom = (row_id == rows - 1) & (z == m - 1)
    conduct = layers + 1

    def film_layer(l, below, first):
        film = X[l]
        above = X[l + 1]
        k = X[conduct]
        prev_row = jnp.where(at_top, film, pltpu.roll(film, 1, axis=0))
        next_row = jnp.where(at_bottom, film, pltpu.roll(film, rows + 7, axis=0))
        lateral = (
            prev_row
            + next_row
            + pltpu.roll(film, 1, axis=1)
            + pltpu.roll(film, width + 127, axis=1)
            - 4.0 * film
        )
        normal = normal_gain * k * (above + below - 2.0 * film)
        if first:
            normal = normal - X[layers + 2] * film
        X[l] = film + advance_flux_film * (k * lateral + normal)
        return film

    @pl.loop(0, FILM_SWEEPS)
    def _(step):
        under = film_layer(0, X[0], True)
        lax.fori_loop(1, layers, lambda l, under: film_layer(l, under, False), under)

    flux = normal_gain * X[conduct, 0:rows, 0:width] * (
        X[layers - 1, 0:rows, 0:width] - X[layers, 0:rows, 0:width]
    )
    own = pl.ds(pl.multiple_of(b * width, width), width)
    to_root = remote(flux_out, heat.at[:, own], flux_send, flux_recv.at[b], {"blk": 0})

    @pl.when(has_lo)
    def _():
        flux_out[...] = flux
        to_root.start()
        heat[...] = jnp.zeros_like(heat)

    @pl.when(b == 0)
    def _():
        heat[:, 0:width] = flux

    film_out[...] = X[0:layers, 0:rows, 0:width]

    @pl.when(b == 0)
    def _():
        for k in range(1, n):
            remote(
                flux_out, heat.at[:, k * width : (k + 1) * width], flux_send, flux_recv.at[k], {"blk": 1}
            ).wait_recv()

    sub = lax.broadcasted_iota(jnp.int32, (8, perim), 0)

    def cell(p, q, d, r, below, above, heated, final):
        part = pl.ds(8 * r, 8)
        c = U[p, d + 1, part, :]
        if r == 0:
            edge = jnp.where(has_up, edge_in[p, 0, pl.ds(d, 1), :], c[0:1, :])
            prev_row = jnp.where(sub == 0, edge, pltpu.roll(c, 1, axis=0))
        else:
            prev_row = U[p, d + 1, pl.ds(8 * r - 1, 8), :]
        if r == tiles - 1:
            edge = jnp.where(has_down, edge_in[p, 1, pl.ds(d, 1), :], c[7:8, :])
            next_row = jnp.where(sub == 7, edge, pltpu.roll(c, 7, axis=0))
        else:
            next_row = U[p, d + 1, pl.ds(8 * r + 1, 8), :]
        lap = (
            U[p, below, part, :]
            + U[p, above, part, :]
            + prev_row
            + next_row
            + pltpu.roll(c, 1, axis=1)
            + pltpu.roll(c, perim - 1, axis=1)
            - 6.0 * c
        )
        h = shell_out[d, part, :] + shell_step * lap
        if heated:
            h = h + shell_step * heat[part, :]
        shell_out[d, part, :] = h
        if final and not heated:
            return
        u = thermal_map(h)
        U[q, d + 1, part, :] = u
        if final:
            return
        if r == 0:
            edge_out[q, 0, pl.ds(d, 1), :] = u[0:1, :]
        if r == tiles - 1:
            edge_out[q, 1, pl.ds(d, 1), :] = u[7:8, :]

    below_first = jnp.where(has_lo, 0, 1)
    above_last = jnp.where(has_hi, depth + 1, depth)

    def sweep(s, final):
        p = lax.rem(s, 2)
        q = 1 - p
        later = s >= 1
        pl.when(has_up & later)(lambda: up_copy(q).wait_send())
        pl.when(has_down & later)(lambda: down_copy(q).wait_send())
        pl.when(has_up)(lambda: down_copy(p).wait_recv())
        pl.when(has_down)(lambda: up_copy(p).wait_recv())
        for r in range(tiles):
            pl.when(has_lo & later)(lambda: lo_copy(q, r).wait_send())
            pl.when(has_lo)(lambda: lo_arrives(p, r))
            cell(p, q, 0, r, below_first, 2, True, final)
            if not final:
                pl.when(has_lo)(lambda: lo_copy(q, r).start())
            pl.when(has_hi & later)(lambda: hi_copy(q, r).wait_send())
            pl.when(has_hi)(lambda: hi_arrives(p, r))
            cell(p, q, depth - 1, r, depth - 1, above_last, False, final)
            if not final:
                pl.when(has_hi)(lambda: hi_copy(q, r).start())
        if final:

            @pl.when(b == 0)
            def _():
                for k in range(1, n):
                    face_copy(k).start()

        @pl.loop(1, depth - 1)
        def _(d):
            cell(p, q, d, 0, d, d + 2, False, final)
            cell(p, q, d, tiles - 1, d, d + 2, False, final)

        if not final:
            pl.when(has_up)(lambda: up_copy(q).start())
            pl.when(has_down)(lambda: down_copy(q).start())

        @pl.loop(1, depth - 1)
        def _(d):
            for r in range(1, tiles - 1):
                cell(p, q, d, r, d, d + 2, False, final)

    end = SHELL_SWEEPS % 2

    def face_copy(k):
        return remote(
            U.at[end, 1, :, k * width : (k + 1) * width], face_in, face_send.at[k], face_recv, {"blk": k}
        )

    @pl.loop(0, SHELL_SWEEPS - 1)
    def _(s):
        sweep(s, False)

    sweep(jnp.int32(SHELL_SWEEPS - 1), True)

    @pl.when(b == 0)
    def _():
        surf_out[...] = U[end, 1, :, 0:width]

    @pl.when(has_lo)
    def _():
        face_copy(1).wait_recv()
        surf_out[...] = face_in[...]

    @pl.when(b == 0)
    def _():
        for k in range(1, n):
            face_copy(k).wait_send()

    q = 1 - end
    col_left.wait_send()
    col_right.wait_send()

    @pl.when(has_up)
    def _():
        row_up.wait_send()
        cor_up.wait_send()
        up_copy(q).wait_send()

    @pl.when(has_down)
    def _():
        row_down.wait_send()
        cor_down.wait_send()
        down_copy(q).wait_send()

    @pl.when(has_lo)
    def _():
        to_root.wait_send()
        for r in range(tiles):
            lo_copy(q, r).wait_send()

    @pl.when(has_hi)
    def _():
        for r in range(tiles):
            hi_copy(q, r).wait_send()


def body(n, m, film_temp, surface_temp, shell_enthalpy, phase_codes, zone_ids, zone_htc):
    layers, rows, width = film_temp.shape
    depth, _, perim = shell_enthalpy.shape
    tiles = rows // 8
    full = layers + 3
    f32 = jnp.float32
    vmem = pl.BlockSpec(memory_space=pltpu.VMEM)
    smem = pl.BlockSpec(memory_space=pltpu.SMEM)
    dma = pltpu.SemaphoreType.DMA
    return pl.pallas_call(
        functools.partial(kernel, n, m),
        out_shape=[
            jax.ShapeDtypeStruct(film_temp.shape, f32),
            jax.ShapeDtypeStruct(shell_enthalpy.shape, f32),
            jax.ShapeDtypeStruct(surface_temp.shape, f32),
        ],
        in_specs=[vmem, vmem, vmem, smem, smem, smem],
        out_specs=[vmem, vmem, vmem],
        scratch_shapes=[
            pltpu.VMEM((full, rows + 8, width + 128), f32),
            pltpu.VMEM((2, rows, 128), f32),
            pltpu.VMEM((2, rows, 128), f32),
            pltpu.VMEM((2, full, W, width), f32),
            pltpu.VMEM((2, full, W, width), f32),
            pltpu.VMEM((2, 2, W, 128), f32),
            pltpu.VMEM((2, 2, W, 128), f32),
            pltpu.VMEM((2, 8, 128), f32),
            pltpu.VMEM((2, depth + 2, rows, perim), f32),
            pltpu.VMEM((2, 2, depth, perim), f32),
            pltpu.VMEM((2, 2, depth, perim), f32),
            pltpu.VMEM((rows, perim), f32),
            pltpu.VMEM((rows, width), f32),
            pltpu.VMEM((rows, width), f32),
            dma((6,)),
            dma((6,)),
            dma(()),
            dma((n,)),
            dma((n,)),
            dma(()),
            dma((2, 2, tiles)),
            dma((2, 2, tiles)),
            dma((2, 2)),
            dma((2, 2)),
        ],
        compiler_params=pltpu.CompilerParams(
            collective_id=0, has_side_effects=True, vmem_limit_bytes=48 * 1024 * 1024
        ),
    )(film_temp, surface_temp, shell_enthalpy, phase_codes, zone_ids, zone_htc)


def solution(mesh):
    placed = (
        P(None, "cast", "blk"),
        P("cast", "blk"),
        P("blk", "cast", None),
        P("cast", "blk"),
        P("cast"),
        P(),
    )
    return jax.shard_map(
        functools.partial(body, mesh.shape["blk"], mesh.shape["cast"]),
        mesh=mesh,
        in_specs=placed,
        out_specs=(P(None, "cast", "blk"), P("blk", "cast", None), P("cast", "blk")),
        check_vma=False,
    )
```

time: 463 us -> 85.7 us (0.19)
  waiting for transfers between devices: 138 us -> 0 us
  starting transfers between devices: 125 us -> 0 us
  local copies, waits for them, and re-layouts: 95.5 us -> 8.1 us
  other arithmetic: 79.3 us -> 0 us
  Pallas kernels: 0 us -> 76.6 us
  between operations: 14.4 us -> 0.65 us
  blocking collectives: 8.34 us -> 0 us
    ppermute x56 -> x0, starting transfers between devices: 125 us -> none  [the longest x28 89.2 us: with_halo(): lax.ppermute(tail, axis, [(i, (i + 1) % count) for i in range(ends)])]
    ppermute x56 -> x0, waiting for transfers between devices: 78.8 us -> none  [the longest x28 65.3 us: with_halo(): lax.ppermute(head, axis, [((i + 1) % count, i) for i in range(ends)])]
    slice x71 -> x0, local copies, waits for them, and re-layouts: 77.3 us -> none  [the longest x24 46.8 us: mirror_ends(): lax.slice_in_dim(trailing_neighbour, 1, length, axis=dim)]
    pallas_call x0 -> x1, Pallas kernels: none -> 76.6 us  [body(): pl.pallas_call(functools.partial(kernel, n, m), out_shape=[jax.ShapeDtype...]
    add x24 -> x0, other arithmetic: 72.3 us -> none  [the longest x10 50.9 us: sweep_depth(): heat_content_per_mass + shell_step * iteration_counter]
    psum x1 -> x0, waiting for transfers between devices: 59.3 us -> none  [broadcast(): return lax.psum(jnp.where(mine, array, jnp.zeros_like(array)), axis)]
    while x60 -> x0, local copies, waits for them, and re-layouts: 13.2 us -> none
    all_gather x1 -> x0, blocking collectives: 8.34 us -> none  [body(): plane = lax.all_gather(flux, 'blk', axis=1, tiled=True)]
  transfers between devices with their start and end apart: 57 -> 0, of which waited for: 33 -> 0; matrix products, arithmetic and copies ran while one was open for 17% -> 0% of each run, Pallas kernels for 0% -> 0%
where the time goes in v1:
time: 85.7 us; the launch traced here: 85.4 us
  Pallas kernels  76.6 us (89%)
  local copies, waits for them, and re-layouts  8.1 us (9%)
    pallas_call x1, Pallas kernels, body(): pl.pallas_call(functools.partial(kernel, n, m), out_shape=[jax.ShapeDtype...  76.6 us
    unnamed x15, local copies, waits for them, and re-layouts  8.1 us

profile of v1, /device:TPU:0, one launch (start us, length us, event | category | flops | bytes accessed | tf_op | source)
XLA Modules:
  0.0 85.4 jit_solution(6053859901074307122)
XLA Ops:
  0.6 0.0 copy-start
  0.6 1.6 %copy-done = f32[8,32,2048]{2,1,0:T(8,128)S(1)} copy-done((f32[8,32,2048]{2,1,0:T(8,128)S(1)}, f32[8,32,2048]{2,1,0:T(8,128)}, u32[]{:S(2)}) %copy-start) | copy-done | bytes 2097176
  2.2 0.0 copy-start.1
  2.2 1.0 %copy-done.1 = f32[16,32,256]{2,1,0:T(8,128)S(1)} copy-done((f32[16,32,256]{2,1,0:T(8,128)S(1)}, f32[16,32,256]{2,1,0:T(8,128)}, u32[]{:S(2)}) %copy-start.1) | copy-done | bytes 524312
  3.3 0.0 copy-start.2
  3.3 0.8 copy-done.2
  4.0 0.0 copy-start.3
  4.0 0.7 copy-done.3
  4.7 0.0 copy-start.4
  4.7 0.7 copy-done.4
  5.4 0.0 copy-start.5
  5.4 0.7 copy-done.5
  6.0 76.6 %shard_map.85 = (f32[16,32,256]{2,1,0:T(8,128)S(1)}, f32[8,32,2048]{2,1,0:T(8,128)S(1)}, f32[32,256]{1,0:T(8,128)S(1)}) custom-call(f32[16,32,256]{2,1,0:T(8,128)S(1)} %copy-done.1, f32[32,256]{1,0:T(8,128)S(1)} %copy-done.2, f32[8,32,2048]{2,1,0:T(8,128)S(1)} %copy-done, s32[4,8]{1,0:T(4,128)S(1)} %copy-done.3, s32[2]{0:T(128)S(1)} %copy-done.4, f32[8]{0:T(128)S(1)} %copy-done.5), custom_call_target="tpu_custom_call" | custom-call | tf_op jit(solution)/shard_map/pallas_call | solution.py:431
  82.7 0.8 copy.12
  83.5 1.3 %copy.13 = f32[8,32,2048]{2,1,0:T(8,128)} copy(f32[8,32,2048]{2,1,0:T(8,128)S(1)} %get-tuple-element.7) | data formatting | bytes 4194304
  84.8 0.6 copy.14
Async XLA Ops:
  0.6 1.6 %copy-start = (f32[8,32,2048]{2,1,0:T(8,128)S(1)}, f32[8,32,2048]{2,1,0:T(8,128)}, u32[]{:S(2)}) copy-start(f32[8,32,2048]{2,1,0:T(8,128)} %shell_ref.1) | copy-start | bytes 6291460
  2.2 1.0 %copy-start.1 = (f32[16,32,256]{2,1,0:T(8,128)S(1)}, f32[16,32,256]{2,1,0:T(8,128)}, u32[]{:S(2)}) copy-start(f32[16,32,256]{2,1,0:T(8,128)} %film_ref.1) | copy-start | bytes 1572868
  3.3 0.8 copy-start.2
  4.0 0.7 copy-start.3
  4.7 0.7 copy-start.4
  5.4 0.7 copy-start.5

commit v2 on v1

--- a/solution.py
+++ b/solution.py
@@ -55,7 +55,8 @@
     corner_out,
     corner_in,
     corner_all,
-    U,
+    UA,
+    UB,
     edge_out,
     edge_in,
     heat,
@@ -72,6 +73,7 @@
     edge_send,
     edge_recv,
 ):
+    U = (UA, UB)
     b = lax.axis_index("blk")
     z = lax.axis_index("cast")
     layers, rows, width = film_ref.shape
@@ -146,13 +148,13 @@
     def lo_copy(p, r):
         part = pl.ds(8 * r, 8)
         return remote(
-            U.at[p, 1, part], U.at[p, depth + 1, part], depth_send.at[p, 0, r], depth_recv.at[p, 1, r], {"blk": b - 1}
+            U[p].at[1, part], U[p].at[depth + 1, part], depth_send.at[p, 0, r], depth_recv.at[p, 1, r], {"blk": b - 1}
         )
 
     def hi_copy(p, r):
         part = pl.ds(8 * r, 8)
         return remote(
-            U.at[p, depth, part], U.at[p, 0, part], depth_send.at[p, 1, r], depth_recv.at[p, 0, r], {"blk": b + 1}
+            U[p].at[depth, part], U[p].at[0, part], depth_send.at[p, 1, r], depth_recv.at[p, 0, r], {"blk": b + 1}
         )
 
     def up_copy(p):
@@ -172,7 +174,7 @@
         h = shell_ref[d, part, :]
         shell_out[d, part, :] = h
         u = thermal_map(h)
-        U[0, d + 1, part, :] = u
+        UA[d + 1, part, :] = u
         if r == 0:
             edge_out[0, 0, pl.ds(d, 1), :] = u[0:1, :]
         if r == tiles - 1:
@@ -286,20 +288,20 @@
 
     def cell(p, q, d, r, below, above, heated, final):
         part = pl.ds(8 * r, 8)
-        c = U[p, d + 1, part, :]
+        c = U[p][d + 1, part, :]
         if r == 0:
             edge = jnp.where(has_up, edge_in[p, 0, pl.ds(d, 1), :], c[0:1, :])
             prev_row = jnp.where(sub == 0, edge, pltpu.roll(c, 1, axis=0))
         else:
-            prev_row = U[p, d + 1, pl.ds(8 * r - 1, 8), :]
+            prev_row = U[p][d + 1, pl.ds(8 * r - 1, 8), :]
         if r == tiles - 1:
             edge = jnp.where(has_down, edge_in[p, 1, pl.ds(d, 1), :], c[7:8, :])
             next_row = jnp.where(sub == 7, edge, pltpu.roll(c, 7, axis=0))
         else:
-            next_row = U[p, d + 1, pl.ds(8 * r + 1, 8), :]
+            next_row = U[p][d + 1, pl.ds(8 * r + 1, 8), :]
         lap = (
-            U[p, below, part, :]
-            + U[p, above, part, :]
+            U[p][below, part, :]
+            + U[p][above, part, :]
             + prev_row
             + next_row
             + pltpu.roll(c, 1, axis=1)
@@ -313,7 +315,7 @@
         if final and not heated:
             return
         u = thermal_map(h)
-        U[q, d + 1, part, :] = u
+        U[q][d + 1, part, :] = u
         if final:
             return
         if r == 0:
@@ -324,25 +326,38 @@
     below_first = jnp.where(has_lo, 0, 1)
     above_last = jnp.where(has_hi, depth + 1, depth)
 
-    def sweep(s, final):
-        p = lax.rem(s, 2)
+    def ends(p, r, later, final):
         q = 1 - p
-        later = s >= 1
+        pl.when(has_lo & later)(lambda: lo_copy(q, r).wait_send())
+        pl.when(has_hi & later)(lambda: hi_copy(q, r).wait_send())
+        pl.when(has_lo)(lambda: lo_arrives(p, r))
+        pl.when(has_hi)(lambda: hi_arrives(p, r))
+        cell(p, q, 0, r, below_first, 2, True, final)
+        cell(p, q, depth - 1, r, depth - 1, above_last, False, final)
+        if not final:
+            pl.when(has_lo)(lambda: lo_copy(q, r).start())
+            pl.when(has_hi)(lambda: hi_copy(q, r).start())
+
+    def sweep(p, later, final):
+        q = 1 - p
+        outer, inner = (0, tiles - 1), range(1, tiles - 1)
         pl.when(has_up & later)(lambda: up_copy(q).wait_send())
         pl.when(has_down & later)(lambda: down_copy(q).wait_send())
         pl.when(has_up)(lambda: down_copy(p).wait_recv())
         pl.when(has_down)(lambda: up_copy(p).wait_recv())
-        for r in range(tiles):
-            pl.when(has_lo & later)(lambda: lo_copy(q, r).wait_send())
-            pl.when(has_lo)(lambda: lo_arrives(p, r))
-            cell(p, q, 0, r, below_first, 2, True, final)
-            if not final:
-                pl.when(has_lo)(lambda: lo_copy(q, r).start())
-            pl.when(has_hi & later)(lambda: hi_copy(q, r).wait_send())
-            pl.when(has_hi)(lambda: hi_arrives(p, r))
-            cell(p, q, depth - 1, r, depth - 1, above_last, False, final)
-            if not final:
-                pl.when(has_hi)(lambda: hi_copy(q, r).start())
+        for r in outer:
+            ends(p, r, later, final)
+
+        @pl.loop(1, depth - 1)
+        def _(d):
+            for r in outer:
+                cell(p, q, d, r, d, d + 2, False, final)
+
+        if not final:
+            pl.when(has_up)(lambda: up_copy(q).start())
+            pl.when(has_down)(lambda: down_copy(q).start())
+        for r in inner:
+            ends(p, r, later, final)
         if final:
 
             @pl.when(b == 0)
@@ -352,34 +367,29 @@
 
         @pl.loop(1, depth - 1)
         def _(d):
-            cell(p, q, d, 0, d, d + 2, False, final)
-            cell(p, q, d, tiles - 1, d, d + 2, False, final)
-
-        if not final:
-            pl.when(has_up)(lambda: up_copy(q).start())
-            pl.when(has_down)(lambda: down_copy(q).start())
-
-        @pl.loop(1, depth - 1)
-        def _(d):
-            for r in range(1, tiles - 1):
+            for r in inner:
                 cell(p, q, d, r, d, d + 2, False, final)
 
     end = SHELL_SWEEPS % 2
 
     def face_copy(k):
         return remote(
-            U.at[end, 1, :, k * width : (k + 1) * width], face_in, face_send.at[k], face_recv, {"blk": k}
-        )
-
-    @pl.loop(0, SHELL_SWEEPS - 1)
-    def _(s):
-        sweep(s, False)
-
-    sweep(jnp.int32(SHELL_SWEEPS - 1), True)
+            U[end].at[1, :, k * width : (k + 1) * width], face_in, face_send.at[k], face_recv, {"blk": k}
+        )
+
+    pairs = (SHELL_SWEEPS - 1) // 2
+
+    @pl.loop(0, pairs)
+    def _(k):
+        sweep(0, k >= 1, False)
+        sweep(1, k >= 0, False)
+
+    for step in range(2 * pairs, SHELL_SWEEPS):
+        sweep(step % 2, has_up | True, step == SHELL_SWEEPS - 1)
 
     @pl.when(b == 0)
     def _():
-        surf_out[...] = U[end, 1, :, 0:width]
+        surf_out[...] = U[end][1, :, 0:width]
 
     @pl.when(has_lo)
     def _():
@@ -446,7 +456,8 @@
             pltpu.VMEM((2, 2, W, 128), f32),
             pltpu.VMEM((2, 2, W, 128), f32),
             pltpu.VMEM((2, 8, 128), f32),
-            pltpu.VMEM((2, depth + 2, rows, perim), f32),
+            pltpu.VMEM((depth + 2, rows, perim), f32),
+            pltpu.VMEM((depth + 2, rows, perim), f32),
             pltpu.VMEM((2, 2, depth, perim), f32),
             pltpu.VMEM((2, 2, depth, perim), f32),
             pltpu.VMEM((rows, perim), f32),

time: 85.7 us -> 80.4 us (0.938)
  the two profiles are of different devices: /device:TPU:0 before, /device:TPU:1 now
where the time goes in v2:
time: 80.4 us; the launch traced here: 80.1 us
  Pallas kernels  71.3 us (89%)
  local copies, waits for them, and re-layouts  8.1 us (10%)
    pallas_call x1, Pallas kernels, body(): pl.pallas_call(functools.partial(kernel, n, m), out_shape=[jax.ShapeDtype...  71.3 us
    unnamed x15, local copies, waits for them, and re-layouts  8.1 us

profile of v2, /device:TPU:1, one launch (start us, length us, event | category | flops | bytes accessed | tf_op | source)
XLA Modules:
  0.0 80.1 jit_solution(151886550357671645)
XLA Ops:
  0.6 0.0 copy-start
  0.6 1.6 %copy-done = f32[8,32,2048]{2,1,0:T(8,128)S(1)} copy-done((f32[8,32,2048]{2,1,0:T(8,128)S(1)}, f32[8,32,2048]{2,1,0:T(8,128)}, u32[]{:S(2)}) %copy-start) | copy-done | bytes 2097176
  2.2 0.0 copy-start.1
  2.2 1.0 %copy-done.1 = f32[16,32,256]{2,1,0:T(8,128)S(1)} copy-done((f32[16,32,256]{2,1,0:T(8,128)S(1)}, f32[16,32,256]{2,1,0:T(8,128)}, u32[]{:S(2)}) %copy-start.1) | copy-done | bytes 524312
  3.3 0.0 copy-start.2
  3.3 0.8 copy-done.2
  4.0 0.0 copy-start.3
  4.0 0.7 copy-done.3
  4.7 0.0 copy-start.4
  4.7 0.7 copy-done.4
  5.4 0.0 copy-start.5
  5.4 0.7 copy-done.5
  6.0 71.3 %shard_map.85 = (f32[16,32,256]{2,1,0:T(8,128)S(1)}, f32[8,32,2048]{2,1,0:T(8,128)S(1)}, f32[32,256]{1,0:T(8,128)S(1)}) custom-call(f32[16,32,256]{2,1,0:T(8,128)S(1)} %copy-done.1, f32[32,256]{1,0:T(8,128)S(1)} %copy-done.2, f32[8,32,2048]{2,1,0:T(8,128)S(1)} %copy-done, s32[4,8]{1,0:T(4,128)S(1)} %copy-done.3, s32[2]{0:T(128)S(1)} %copy-done.4, f32[8]{0:T(128)S(1)} %copy-done.5), custom_call_target="tpu_custom_call" | custom-call | tf_op jit(solution)/shard_map/pallas_call | solution.py:441
  77.3 0.8 copy.12
  78.1 1.3 %copy.13 = f32[8,32,2048]{2,1,0:T(8,128)} copy(f32[8,32,2048]{2,1,0:T(8,128)S(1)} %get-tuple-element.7) | data formatting | bytes 4194304
  79.5 0.6 copy.14
Async XLA Ops:
  0.6 1.6 %copy-start = (f32[8,32,2048]{2,1,0:T(8,128)S(1)}, f32[8,32,2048]{2,1,0:T(8,128)}, u32[]{:S(2)}) copy-start(f32[8,32,2048]{2,1,0:T(8,128)} %shell_ref.1) | copy-start | bytes 6291460
  2.2 1.0 %copy-start.1 = (f32[16,32,256]{2,1,0:T(8,128)S(1)}, f32[16,32,256]{2,1,0:T(8,128)}, u32[]{:S(2)}) copy-start(f32[16,32,256]{2,1,0:T(8,128)} %film_ref.1) | copy-start | bytes 1572868
  3.3 0.8 copy-start.2
  4.0 0.7 copy-start.3
  4.7 0.7 copy-start.4
  5.4 0.7 copy-start.5

commit v3 on v2

--- a/solution.py
+++ b/solution.py
@@ -257,7 +257,8 @@
     @pl.loop(0, FILM_SWEEPS)
     def _(step):
         under = film_layer(0, X[0], True)
-        lax.fori_loop(1, layers, lambda l, under: film_layer(l, under, False), under)
+        for l in range(1, layers):
+            under = film_layer(l, under, False)
 
     flux = normal_gain * X[conduct, 0:rows, 0:width] * (
         X[layers - 1, 0:rows, 0:width] - X[layers, 0:rows, 0:width]

time: 80.4 us -> 76.1 us (0.947)
  Pallas kernels: 71.3 us -> 67 us
    pallas_call x1, Pallas kernels: 71.3 us -> 67 us  [body(): pl.pallas_call(functools.partial(kernel, n, m), out_shape=[jax.ShapeDtype...]
where the time goes in v3:
time: 76.1 us; the launch traced here: 75.7 us
  Pallas kernels  67 us (88%)
  local copies, waits for them, and re-layouts  8.1 us (11%)
    pallas_call x1, Pallas kernels, body(): pl.pallas_call(functools.partial(kernel, n, m), out_shape=[jax.ShapeDtype...  67 us
    unnamed x15, local copies, waits for them, and re-layouts  8.1 us

profile of v3, /device:TPU:1, one launch (start us, length us, event | category | flops | bytes accessed | tf_op | source)
XLA Modules:
  0.0 75.7 jit_solution(14487130263597875406)
XLA Ops:
  0.6 0.0 copy-start
  0.6 1.6 %copy-done = f32[8,32,2048]{2,1,0:T(8,128)S(1)} copy-done((f32[8,32,2048]{2,1,0:T(8,128)S(1)}, f32[8,32,2048]{2,1,0:T(8,128)}, u32[]{:S(2)}) %copy-start) | copy-done | bytes 2097176
  2.2 0.0 copy-start.1
  2.2 1.0 %copy-done.1 = f32[16,32,256]{2,1,0:T(8,128)S(1)} copy-done((f32[16,32,256]{2,1,0:T(8,128)S(1)}, f32[16,32,256]{2,1,0:T(8,128)}, u32[]{:S(2)}) %copy-start.1) | copy-done | bytes 524312
  3.3 0.0 copy-start.2
  3.3 0.8 copy-done.2
  4.0 0.0 copy-start.3
  4.0 0.7 copy-done.3
  4.7 0.0 copy-start.4
  4.7 0.7 copy-done.4
  5.4 0.0 copy-start.5
  5.4 0.7 copy-done.5
  6.0 67.0 %shard_map.85 = (f32[16,32,256]{2,1,0:T(8,128)S(1)}, f32[8,32,2048]{2,1,0:T(8,128)S(1)}, f32[32,256]{1,0:T(8,128)S(1)}) custom-call(f32[16,32,256]{2,1,0:T(8,128)S(1)} %copy-done.1, f32[32,256]{1,0:T(8,128)S(1)} %copy-done.2, f32[8,32,2048]{2,1,0:T(8,128)S(1)} %copy-done, s32[4,8]{1,0:T(4,128)S(1)} %copy-done.3, s32[2]{0:T(128)S(1)} %copy-done.4, f32[8]{0:T(128)S(1)} %copy-done.5), custom_call_target="tpu_custom_call" | custom-call | tf_op jit(solution)/shard_map/pallas_call | solution.py:442
  73.0 0.8 %copy.12 = f32[16,32,256]{2,1,0:T(8,128)} copy(f32[16,32,256]{2,1,0:T(8,128)S(1)} %get-tuple-element.6) | data formatting | bytes 1048576
  73.8 1.3 %copy.13 = f32[8,32,2048]{2,1,0:T(8,128)} copy(f32[8,32,2048]{2,1,0:T(8,128)S(1)} %get-tuple-element.7) | data formatting | bytes 4194304
  75.1 0.6 copy.14
Async XLA Ops:
  0.6 1.6 %copy-start = (f32[8,32,2048]{2,1,0:T(8,128)S(1)}, f32[8,32,2048]{2,1,0:T(8,128)}, u32[]{:S(2)}) copy-start(f32[8,32,2048]{2,1,0:T(8,128)} %shell_ref.1) | copy-start | bytes 6291460
  2.2 1.0 %copy-start.1 = (f32[16,32,256]{2,1,0:T(8,128)S(1)}, f32[16,32,256]{2,1,0:T(8,128)}, u32[]{:S(2)}) copy-start(f32[16,32,256]{2,1,0:T(8,128)} %film_ref.1) | copy-start | bytes 1572868
  3.3 0.8 %copy-start.2 = (f32[32,256]{1,0:T(8,128)S(1)}, f32[32,256]{1,0:T(8,128)}, u32[]{:S(2)}) copy-start(f32[32,256]{1,0:T(8,128)} %surf_ref.1) | copy-start | bytes 98308
  4.0 0.7 copy-start.3
  4.7 0.7 copy-start.4
  5.4 0.7 copy-start.5

commit v4 on v2

--- a/solution.py
+++ b/solution.py
@@ -72,6 +72,7 @@
     depth_recv,
     edge_send,
     edge_recv,
+    load_sem,
 ):
     U = (UA, UB)
     b = lax.axis_index("blk")
@@ -84,6 +85,14 @@
     has_up, has_down = z > 0, z < m - 1
     has_lo, has_hi = b > 0, b < n - 1
 
+    loads = (
+        pltpu.make_async_copy(film_ref, X.at[0:layers, 0:rows, 0:width], load_sem.at[0]),
+        pltpu.make_async_copy(surf_ref, X.at[layers, 0:rows, 0:width], load_sem.at[1]),
+        pltpu.make_async_copy(shell_ref, shell_out, load_sem.at[2]),
+    )
+    for load in loads:
+        load.start()
+
     barrier = pltpu.get_barrier_semaphore()
     for k in range(1, n):
         pl.semaphore_signal(
@@ -99,8 +108,6 @@
         pl.semaphore_signal(barrier, inc=1, device_id={"cast": z + 1}, device_id_type=pl.DeviceIdType.MESH)
 
     lane = lax.broadcasted_iota(jnp.int32, (8, width), 1)
-    X[0:layers, 0:rows, 0:width] = film_ref[...]
-    X[layers, 0:rows, 0:width] = surf_ref[...]
     for i in range(tiles):
         values = jnp.zeros((8, width), jnp.float32)
         for j in range(width // TILE_P):
@@ -118,6 +125,8 @@
         )
     X[:, rows : rows + 8, :] = jnp.zeros((full, 8, width + 128), jnp.float32)
 
+    loads[0].wait()
+    loads[1].wait()
     lane_r = lax.broadcasted_iota(jnp.int32, (rows, 128), 1)
     first = jnp.zeros((rows, 128), jnp.float32)
     last = jnp.zeros((rows, 128), jnp.float32)
@@ -169,10 +178,11 @@
     def hi_arrives(p, r):
         lo_copy(p, r).wait_recv()
 
+    loads[2].wait()
+
     def first_step(d, r):
         part = pl.ds(8 * r, 8)
-        h = shell_ref[d, part, :]
-        shell_out[d, part, :] = h
+        h = shell_out[d, part, :]
         u = thermal_map(h)
         UA[d + 1, part, :] = u
         if r == 0:
@@ -253,36 +263,6 @@
             normal = normal - X[layers + 2] * film
         X[l] = film + advance_flux_film * (k * lateral + normal)
         return film
-
-    @pl.loop(0, FILM_SWEEPS)
-    def _(step):
-        under = film_layer(0, X[0], True)
-        lax.fori_loop(1, layers, lambda l, under: film_layer(l, under, False), under)
-
-    flux = normal_gain * X[conduct, 0:rows, 0:width] * (
-        X[layers - 1, 0:rows, 0:width] - X[layers, 0:rows, 0:width]
-    )
-    own = pl.ds(pl.multiple_of(b * width, width), width)
-    to_root = remote(flux_out, heat.at[:, own], flux_send, flux_recv.at[b], {"blk": 0})
-
-    @pl.when(has_lo)
-    def _():
-        flux_out[...] = flux
-        to_root.start()
-        heat[...] = jnp.zeros_like(heat)
-
-    @pl.when(b == 0)
-    def _():
-        heat[:, 0:width] = flux
-
-    film_out[...] = X[0:layers, 0:rows, 0:width]
-
-    @pl.when(b == 0)
-    def _():
-        for k in range(1, n):
-            remote(
-                flux_out, heat.at[:, k * width : (k + 1) * width], flux_send, flux_recv.at[k], {"blk": 1}
-            ).wait_recv()
 
     sub = lax.broadcasted_iota(jnp.int32, (8, perim), 0)
 
@@ -326,19 +306,19 @@
     below_first = jnp.where(has_lo, 0, 1)
     above_last = jnp.where(has_hi, depth + 1, depth)
 
-    def ends(p, r, later, final):
+    def ends(p, r, later, final, early):
         q = 1 - p
         pl.when(has_lo & later)(lambda: lo_copy(q, r).wait_send())
         pl.when(has_hi & later)(lambda: hi_copy(q, r).wait_send())
         pl.when(has_lo)(lambda: lo_arrives(p, r))
         pl.when(has_hi)(lambda: hi_arrives(p, r))
-        cell(p, q, 0, r, below_first, 2, True, final)
+        cell(p, q, 0, r, below_first, 2, not early, final)
         cell(p, q, depth - 1, r, depth - 1, above_last, False, final)
         if not final:
             pl.when(has_lo)(lambda: lo_copy(q, r).start())
             pl.when(has_hi)(lambda: hi_copy(q, r).start())
 
-    def sweep(p, later, final):
+    def sweep(p, later, final, early=False):
         q = 1 - p
         outer, inner = (0, tiles - 1), range(1, tiles - 1)
         pl.when(has_up & later)(lambda: up_copy(q).wait_send())
@@ -346,7 +326,7 @@
         pl.when(has_up)(lambda: down_copy(p).wait_recv())
         pl.when(has_down)(lambda: up_copy(p).wait_recv())
         for r in outer:
-            ends(p, r, later, final)
+            ends(p, r, later, final, early)
 
         @pl.loop(1, depth - 1)
         def _(d):
@@ -354,10 +334,11 @@
                 cell(p, q, d, r, d, d + 2, False, final)
 
         if not final:
-            pl.when(has_up)(lambda: up_copy(q).start())
-            pl.when(has_down)(lambda: down_copy(q).start())
+            ready = has_lo if early else has_lo | True
+            pl.when(has_up & ready)(lambda: up_copy(q).start())
+            pl.when(has_down & ready)(lambda: down_copy(q).start())
         for r in inner:
-            ends(p, r, later, final)
+            ends(p, r, later, final, early)
         if final:
 
             @pl.when(b == 0)
@@ -377,14 +358,59 @@
             U[end].at[1, :, k * width : (k + 1) * width], face_in, face_send.at[k], face_recv, {"blk": k}
         )
 
-    pairs = (SHELL_SWEEPS - 1) // 2
+    sweep(0, has_up & False, False, True)
+
+    @pl.loop(0, FILM_SWEEPS)
+    def _(step):
+        under = film_layer(0, X[0], True)
+        for l in range(1, layers):
+            under = film_layer(l, under, False)
+
+    flux = normal_gain * X[conduct, 0:rows, 0:width] * (
+        X[layers - 1, 0:rows, 0:width] - X[layers, 0:rows, 0:width]
+    )
+    own = pl.ds(pl.multiple_of(b * width, width), width)
+    to_root = remote(flux_out, heat.at[:, own], flux_send, flux_recv.at[b], {"blk": 0})
+
+    @pl.when(has_lo)
+    def _():
+        flux_out[...] = flux
+        to_root.start()
+        heat[...] = jnp.zeros_like(heat)
+
+    @pl.when(b == 0)
+    def _():
+        heat[:, 0:width] = flux
+
+    film_out[...] = X[0:layers, 0:rows, 0:width]
+
+    @pl.when(b == 0)
+    def _():
+        for k in range(1, n):
+            remote(
+                flux_out, heat.at[:, k * width : (k + 1) * width], flux_send, flux_recv.at[k], {"blk": 1}
+            ).wait_recv()
+        for r in range(tiles):
+            part = pl.ds(8 * r, 8)
+            h = shell_out[0, part, :] + shell_step * heat[part, :]
+            shell_out[0, part, :] = h
+            u = thermal_map(h)
+            UB[1, part, :] = u
+            if r == 0:
+                edge_out[1, 0, 0:1, :] = u[0:1, :]
+            if r == tiles - 1:
+                edge_out[1, 1, 0:1, :] = u[7:8, :]
+        pl.when(has_up)(lambda: up_copy(1).start())
+        pl.when(has_down)(lambda: down_copy(1).start())
+
+    pairs = (SHELL_SWEEPS - 2) // 2
 
     @pl.loop(0, pairs)
     def _(k):
-        sweep(0, k >= 1, False)
         sweep(1, k >= 0, False)
-
-    for step in range(2 * pairs, SHELL_SWEEPS):
+        sweep(0, k >= 0, False)
+
+    for step in range(2 * pairs + 1, SHELL_SWEEPS):
         sweep(step % 2, has_up | True, step == SHELL_SWEEPS - 1)
 
     @pl.when(b == 0)
@@ -436,6 +462,7 @@
     full = layers + 3
     f32 = jnp.float32
     vmem = pl.BlockSpec(memory_space=pltpu.VMEM)
+    hbm = pl.BlockSpec(memory_space=pl.ANY)
     smem = pl.BlockSpec(memory_space=pltpu.SMEM)
     dma = pltpu.SemaphoreType.DMA
     return pl.pallas_call(
@@ -445,7 +472,7 @@
             jax.ShapeDtypeStruct(shell_enthalpy.shape, f32),
             jax.ShapeDtypeStruct(surface_temp.shape, f32),
         ],
-        in_specs=[vmem, vmem, vmem, smem, smem, smem],
+        in_specs=[hbm, hbm, hbm, smem, smem, smem],
         out_specs=[vmem, vmem, vmem],
         scratch_shapes=[
             pltpu.VMEM((full, rows + 8, width + 128), f32),
@@ -473,9 +500,10 @@
             dma((2, 2, tiles)),
             dma((2, 2)),
             dma((2, 2)),
+            dma((3,)),
         ],
         compiler_params=pltpu.CompilerParams(
-            collective_id=0, has_side_effects=True, vmem_limit_bytes=48 * 1024 * 1024
+            collective_id=0, has_side_effects=True, vmem_limit_bytes=60 * 1024 * 1024
         ),
     )(film_temp, surface_temp, shell_enthalpy, phase_codes, zone_ids, zone_htc)
 

time: 80.4 us -> 75.1 us (0.934)
  the two profiles are of different devices: /device:TPU:1 before, /device:TPU:0 now
where the time goes in v4:
time: 75.1 us; the launch traced here: 74.9 us
  Pallas kernels  68.6 us (91%)
  local copies, waits for them, and re-layouts  5.64 us (8%)
    pallas_call x1, Pallas kernels, body(): pl.pallas_call(functools.partial(kernel, n, m), out_shape=[jax.ShapeDtype...  68.6 us
    unnamed x5, local copies, waits for them, and re-layouts  5.64 us

profile of v4, /device:TPU:0, one launch (start us, length us, event | category | flops | bytes accessed | tf_op | source)
XLA Modules:
  0.0 74.9 jit_solution(1533371679882500221)
XLA Ops:
  0.6 68.6 %shard_map.85 = (f32[16,32,256]{2,1,0:T(8,128)}, f32[8,32,2048]{2,1,0:T(8,128)}, f32[32,256]{1,0:T(8,128)}) custom-call(f32[16,32,256]{2,1,0:T(8,128)} %film_ref.1, f32[32,256]{1,0:T(8,128)} %surf_ref.1, f32[8,32,2048]{2,1,0:T(8,128)} %shell_ref.1, s32[4,8]{1,0:T(4,128)} %codes_ref.1, s32[2]{0:T(128)} %zone_ref.1, f32[8]{0:T(128)} %htc_ref.1), custom_call_target="tpu_custom_call" | custom-call | tf_op jit(solution)/shard_map/pallas_call | solution.py:468
  69.2 1.9 %copy.12 = f32[16,32,256]{2,1,0:T(8,128)} copy(f32[16,32,256]{2,1,0:T(8,128)} %get-tuple-element.6) | data formatting | bytes 1048576
  71.1 0.0 copy-start
  71.1 3.1 %copy.13 = f32[8,32,2048]{2,1,0:T(8,128)} copy(f32[8,32,2048]{2,1,0:T(8,128)} %get-tuple-element.7) | data formatting | bytes 4194304
  74.2 0.0 copy-done
  74.3 0.6 copy.14
Async XLA Ops:
  71.1 3.1 %copy-start = (f32[32,256]{1,0:T(8,128)S(1)}, f32[32,256]{1,0:T(8,128)}, u32[]{:S(2)}) copy-start(f32[32,256]{1,0:T(8,128)} %get-tuple-element.8) | copy-start | bytes 98308
